TPU v7x, 256 devices: a whole 4x4x8 slice. The times are simulated.
256 devices in a mesh: seq: 64 (over z, x, core), chan: 4 (over y).
Axes of the slice: x: 4, y: 4, z: 8, core: 2. Of those that a mesh axis runs over, the one named last changes fastest.
Arguments:
- proj_query: float32 [32768, 2048], P('seq', 'chan'), may hold values from -6 to 6
- proj_key: float32 [32768, 2048], P('seq', 'chan'), may hold values from -6 to 6
- proj_value: float32 [32768, 2048], P('seq', 'chan'), may hold values from -6 to 6
- long_filter: float32 [32768, 2048], P('seq', 'chan'), may hold values from -0.03125 to 0.03125
- short_weight: float32 [3, 3, 2048], P(None, None, 'chan'), may hold values from -6.3 to 6.3
- skip_gain: float32 [2048], P('chan'), may hold values from -4 to 4
Outputs:
- mixed: float32 [32768, 2048], P('seq', 'chan')
All inputs are finite; a program needn't handle non-finite values.
Results may differ from a plain program's by a relative error of at most 0.00011.
Values sent between devices are 32-bit elements; how exact they have to be, the bound alone decides.
No kernel may reach another device: no remote copies, remote signals or barrier semaphores. Data moves between devices by JAX's collectives and lax.ppermute only.
A program may use at most 64 MiB of HBM per device.

v0:
```python
import math

import jax
import jax.numpy as jnp
from jax import lax
from jax.sharding import PartitionSpec as P


def from_behind(value, axis, steps):
    count = lax.axis_size(axis)
    pairs = [(source, (source + steps) % count) for source in range(count)]
    return lax.ppermute(value, axis, pairs)


def angles(first, second, period):
    turns = first[:, None] * second[None, :] % period
    return 2.0 * math.pi / period * turns.astype(jnp.float32)


def apply_table(table, values):
    return jnp.dot(
        table, values, precision=lax.Precision.HIGHEST, preferred_element_type=jnp.float32
    )


def per_device(proj_query, proj_key, proj_value, long_filter, short_weight, skip_gain):
    seq_local = proj_query.shape[0]
    chan_width = proj_query.shape[1]
    shards = lax.axis_size("seq")
    rows_each = seq_local // shards
    seq_total = seq_local * shards
    position = lax.axis_index("seq")
    stacked = jnp.stack([proj_query, proj_key, proj_value])
    previous = from_behind(stacked[:, seq_local - 2 :, :], "seq", 1)
    extended = jnp.concatenate([previous, stacked], axis=1)
    filtered = (
        short_weight[0][:, None, :] * stacked
        + short_weight[1][:, None, :] * extended[:, 1 : seq_local + 1, :]
        + short_weight[2][:, None, :] * extended[:, :seq_local, :]
    )
    gated_query = filtered[0]
    product = filtered[1] * filtered[2]
    indices = jnp.arange(shards, dtype=jnp.int32)
    small_angle = angles(indices, indices, shards)
    cos_small = jnp.cos(small_angle)
    sin_small = jnp.sin(small_angle)
    local_rows = jnp.arange(seq_local, dtype=jnp.int32)
    big_angle = angles(local_rows, local_rows, seq_local)
    cos_big = jnp.cos(big_angle)
    sin_big = jnp.sin(big_angle)

    def second_section(real_in, imag_in, columns):
        real_flat = real_in.reshape(seq_local, columns)
        imag_flat = imag_in.reshape(seq_local, columns)
        out_real = apply_table(cos_big, real_flat) + apply_table(sin_big, imag_flat)
        out_imag = apply_table(cos_big, imag_flat) - apply_table(sin_big, real_flat)
        return (out_real, out_imag)

    signal_cols, filter_cols = (
        lax.all_to_all(product, "seq", split_axis=0, concat_axis=0, tiled=True),
        lax.all_to_all(long_filter, "seq", split_axis=0, concat_axis=0, tiled=True),
    )
    sub_rows = position * rows_each + jnp.arange(rows_each, dtype=jnp.int32)
    twist = angles(indices, sub_rows, seq_total)
    twist_cos = jnp.cos(twist)[:, :, None]
    twist_sin = jnp.sin(twist)[:, :, None]

    def first_section(columns):
        flat = columns.reshape(shards, rows_each * chan_width)
        real_part = apply_table(cos_small, flat).reshape(shards, rows_each, chan_width)
        imag_part = -apply_table(sin_small, flat).reshape(shards, rows_each, chan_width)
        turned_real = real_part * twist_cos + imag_part * twist_sin
        turned_imag = imag_part * twist_cos - real_part * twist_sin
        return (turned_real, turned_imag)

    signal_real, signal_imag = first_section(signal_cols)
    filter_real, filter_imag = first_section(filter_cols)
    gathered = (
        lax.all_to_all(signal_real, "seq", split_axis=0, concat_axis=1, tiled=True),
        lax.all_to_all(signal_imag, "seq", split_axis=0, concat_axis=1, tiled=True),
        lax.all_to_all(filter_real, "seq", split_axis=0, concat_axis=1, tiled=True),
        lax.all_to_all(filter_imag, "seq", split_axis=0, concat_axis=1, tiled=True),
    )
    spec_real, spec_imag = second_section(gathered[0], gathered[1], chan_width)
    filt_real, filt_imag = second_section(gathered[2], gathered[3], chan_width)
    sorted_parts = (
        lax.all_to_all(spec_real, "seq", split_axis=0, concat_axis=0, tiled=True),
        lax.all_to_all(spec_imag, "seq", split_axis=0, concat_axis=0, tiled=True),
        lax.all_to_all(filt_real, "seq", split_axis=0, concat_axis=0, tiled=True),
        lax.all_to_all(filt_imag, "seq", split_axis=0, concat_axis=0, tiled=True),
    )

    def into_order(values):
        return jnp.transpose(values.reshape(shards, rows_each, chan_width), (1, 0, 2)).reshape(
            seq_local, chan_width
        )

    def out_of_order(values):
        return jnp.transpose(values.reshape(rows_each, shards, chan_width), (1, 0, 2)).reshape(
            seq_local, chan_width
        )

    ordered = [into_order(values) for values in sorted_parts]
    joint_real = ordered[0] * ordered[2] - ordered[1] * ordered[3]
    joint_imag = ordered[0] * ordered[3] + ordered[1] * ordered[2]
    freq_real, freq_imag = (
        lax.all_to_all(out_of_order(joint_real), "seq", split_axis=0, concat_axis=0, tiled=True),
        lax.all_to_all(out_of_order(joint_imag), "seq", split_axis=0, concat_axis=0, tiled=True),
    )
    back_real = apply_table(cos_big, freq_real) - apply_table(sin_big, freq_imag)
    back_imag = apply_table(cos_big, freq_imag) + apply_table(sin_big, freq_real)
    back_turns = local_rows * position % seq_total
    back_angle = 2.0 * math.pi / seq_total * back_turns.astype(jnp.float32)
    back_cos = jnp.cos(back_angle)[:, None]
    back_sin = jnp.sin(back_angle)[:, None]
    turned_real = back_real * back_cos - back_imag * back_sin
    turned_imag = back_real * back_sin + back_imag * back_cos
    split_real, split_imag = (
        lax.all_to_all(turned_real, "seq", split_axis=0, concat_axis=0, tiled=True),
        lax.all_to_all(turned_imag, "seq", split_axis=0, concat_axis=0, tiled=True),
    )
    flat_real = split_real.reshape(shards, rows_each * chan_width)
    flat_imag = split_imag.reshape(shards, rows_each * chan_width)
    inverse_block = (
        apply_table(cos_small, flat_real) - apply_table(sin_small, flat_imag)
    ) / seq_total
    inverse_block = inverse_block.reshape(shards, rows_each, chan_width)
    convolved = lax.all_to_all(
        inverse_block, "seq", split_axis=0, concat_axis=1, tiled=True
    ).reshape(seq_local, chan_width)
    response = gated_query * (convolved + skip_gain[None, :] * product)
    energy = lax.psum(jnp.sum(response * response, axis=1), "chan")
    mean_energy = energy / (chan_width * lax.axis_size("chan"))
    return response / jnp.sqrt(mean_energy[:, None] + 1e-06)


def solution(mesh):
    return jax.shard_map(
        per_device,
        mesh=mesh,
        in_specs=(
            P("seq", "chan"),
            P("seq", "chan"),
            P("seq", "chan"),
            P("seq", "chan"),
            P(None, None, "chan"),
            P("chan"),
        ),
        out_specs=P("seq", "chan"),
        check_vma=False,
    )
```

profile of v0, /device:TPU:24, one launch (start us, length us, event | category | flops | bytes accessed | tf_op | source)
XLA Modules:
  0.0 580.1 jit_solution(17900894150027192388)
XLA Ops:
  0.0 12.2 %all-to-all-start.4 = ((f32[64,8,512]{2,1,0:T(8,128)}), f32[64,8,512]{2,1,0:T(8,128)}, u32[]{:S(2)}, u32[]{:S(2)}) async-start(f32[64,8,512]{2,1,0:T(8,128)} %bitcast.137), calls=%async_computation.4 | async-start | bytes 2097152 | tf_op jit(solution)/shard_map/all_to_all | solution.py:61
  14.7 23.1 %collective-permute-done = f32[3,2,512]{2,1,0:T(2,128)S(1)} collective-permute-done((f32[3,2,512]{2,1,0:T(2,128)S(1)}, f32[3,2,512]{2,1,0:T(2,128)S(1)}, u32[]{:S(2)}, u32[]{:S(2)}) %collective-permute-start) | collective-permute-done | bytes 12320 | tf_op jit(solution)/shard_map/ppermute | solution.py:12
  40.9 7.9 %all-to-all-start = ((f32[64,8,512]{2,1,0:T(8,128)}), f32[64,8,512]{2,1,0:T(8,128)}, u32[]{:S(2)}, u32[]{:S(2)}) async-start(f32[64,8,512]{2,1,0:T(8,128)} %fusion.57), calls=%async_computation | async-start | bytes 2097152 | tf_op jit(solution)/shard_map/all_to_all | solution.py:60
  52.8 24.8 %all-to-all-done = f32[64,8,512]{2,1,0:T(8,128)} async-done(((f32[64,8,512]{2,1,0:T(8,128)}), f32[64,8,512]{2,1,0:T(8,128)}, u32[]{:S(2)}, u32[]{:S(2)}) %all-to-all-start) | async-done | bytes 1048608 | tf_op jit(solution)/shard_map/all_to_all | solution.py:60
  98.6 25.9 %all-to-all-done.6 = f32[64,8,512]{2,1,0:T(8,128)} async-done(((f32[64,8,512]{2,1,0:T(8,128)}), f32[64,8,512]{2,1,0:T(8,128)}, u32[]{:S(2)}, u32[]{:S(2)}) %all-to-all-start.6) | async-done | bytes 1048608 | tf_op jit(solution)/shard_map/all_to_all | solution.py:82
  133.1 25.9 %all-to-all-done.5 = f32[64,8,512]{2,1,0:T(8,128)} async-done(((f32[64,8,512]{2,1,0:T(8,128)}), f32[64,8,512]{2,1,0:T(8,128)}, u32[]{:S(2)}, u32[]{:S(2)}) %all-to-all-start.5) | async-done | bytes 1048608 | tf_op jit(solution)/shard_map/all_to_all | solution.py:81
  167.9 25.9 %all-to-all-done.2 = f32[64,8,512]{2,1,0:T(8,128)} async-done(((f32[64,8,512]{2,1,0:T(8,128)}), f32[64,8,512]{2,1,0:T(8,128)}, u32[]{:S(2)}, u32[]{:S(2)}) %all-to-all-start.2) | async-done | bytes 1048608 | tf_op jit(solution)/shard_map/all_to_all | solution.py:80
  206.5 8.0 %fusion.5 = f32[64,8,512]{2,1,0:T(8,128)} fusion(f32[512,512]{1,0:T(8,128)S(1)} %fusion.28, f32[64,8,512]{2,1,0:T(8,128)} %all-to-all-done.6), kind=kOutput, calls=%fused_computation.18 | convolution fusion | flops 1614544896 | bytes 3145728 | tf_op jit(solution)/shard_map/dot_general | solution.py:21
  214.5 13.8 %all-to-all-done.1 = f32[64,8,512]{2,1,0:T(8,128)} async-done(((f32[64,8,512]{2,1,0:T(8,128)}), f32[64,8,512]{2,1,0:T(8,128)}, u32[]{:S(2)}, u32[]{:S(2)}) %all-to-all-start.1) | async-done | bytes 1048608 | tf_op jit(solution)/shard_map/all_to_all | solution.py:79
  241.2 7.9 %fusion.3 = f32[64,8,512]{2,1,0:T(8,128)} fusion(f32[512,512]{1,0:T(8,128)S(1)} %fusion.24, f32[64,8,512]{2,1,0:T(8,128)} %all-to-all-done.5), kind=kOutput, calls=%fused_computation.14 | convolution fusion | flops 1614544896 | bytes 3145728 | tf_op jit(solution)/shard_map/dot_general | solution.py:21
  249.1 13.9 %all-to-all-done.7 = f32[64,8,512]{2,1,0:T(8,128)} async-done(((f32[64,8,512]{2,1,0:T(8,128)}), f32[64,8,512]{2,1,0:T(8,128)}, u32[]{:S(2)}, u32[]{:S(2)}) %all-to-all-start.7) | async-done | bytes 1048608 | tf_op jit(solution)/shard_map/all_to_all | solution.py:89
  275.9 8.0 %fusion.6 = f32[64,8,512]{2,1,0:T(8,128)} fusion(f32[512,512]{1,0:T(8,128)S(1)} %fusion.34, f32[64,8,512]{2,1,0:T(8,128)} %all-to-all-done.2), kind=kOutput, calls=%fused_computation.21 | convolution fusion | flops 1614544896 | bytes 3145728 | tf_op jit(solution)/shard_map/dot_general | solution.py:21
  283.9 13.9 %all-to-all-done.9 = f32[64,8,512]{2,1,0:T(8,128)} async-done(((f32[64,8,512]{2,1,0:T(8,128)}), f32[64,8,512]{2,1,0:T(8,128)}, u32[]{:S(2)}, u32[]{:S(2)}) %all-to-all-start.9) | async-done | bytes 1048608 | tf_op jit(solution)/shard_map/all_to_all | solution.py:90
  310.6 7.9 %fusion.4 = f32[64,8,512]{2,1,0:T(8,128)} fusion(f32[512,512]{1,0:T(8,128)S(1)} %fusion.30, f32[64,8,512]{2,1,0:T(8,128)} %all-to-all-done.1), kind=kOutput, calls=%fused_computation.16 | convolution fusion | flops 1614544896 | bytes 3145728 | tf_op jit(solution)/shard_map/dot_general | solution.py:21
  318.5 13.9 %all-to-all-done.3 = f32[64,8,512]{2,1,0:T(8,128)} async-done(((f32[64,8,512]{2,1,0:T(8,128)}), f32[64,8,512]{2,1,0:T(8,128)}, u32[]{:S(2)}, u32[]{:S(2)}) %all-to-all-start.3) | async-done | bytes 1048608 | tf_op jit(solution)/shard_map/all_to_all | solution.py:87
  332.4 34.5 %all_to_all.132 = f32[64,8,512]{2,1,0:T(8,128)S(1)} all-to-all(f32[64,8,512]{2,1,0:T(8,128)} %fusion.4), channel_id=1, replica_groups=mesh['seq'=64,'chan'=4] {'seq'}, dimensions={0} | all-to-all | bytes 2097152 | tf_op jit(solution)/shard_map/all_to_all | solution.py:88
  370.2 34.3 %all_to_all.133 = f32[64,8,512]{2,1,0:T(8,128)} all-to-all(f32[64,8,512]{2,1,0:T(8,128)S(1)} %get-tuple-element.8), channel_id=1, replica_groups=mesh['seq'=64,'chan'=4] {'seq'}, dimensions={0} | all-to-all | bytes 2097152 | tf_op jit(solution)/shard_map/all_to_all | solution.py:108
  410.6 7.9 %fusion.18 = f32[512,512]{1,0:T(8,128)} fusion(f32[64,8,512]{2,1,0:T(8,128)} %all_to_all.133), kind=kOutput, calls=%fused_computation.37 | convolution fusion | flops 1614282752 | bytes 2097152 | tf_op jit(solution)/shard_map/dot_general | solution.py:21
  418.5 20.6 %all-to-all-done.10 = f32[64,8,512]{2,1,0:T(8,128)} async-done(((f32[64,8,512]{2,1,0:T(8,128)}), f32[64,8,512]{2,1,0:T(8,128)}, u32[]{:S(2)}, u32[]{:S(2)}) %all-to-all-start.10) | async-done | bytes 1048608 | tf_op jit(solution)/shard_map/all_to_all | solution.py:107
  446.1 7.2 %convolution_add_fusion = f32[512,512]{1,0:T(8,128)S(1)} fusion(f32[512,512]{1,0:T(8,128)S(1)} %copy-done.8, f32[64,8,512]{2,1,0:T(8,128)} %all-to-all-done.10), kind=kOutput, calls=%fused_computation.11 | convolution fusion | flops 1614544896 | bytes 3145728 | tf_op jit(solution)/shard_map/dot_general | solution.py:21
  460.4 34.3 %all_to_all.134 = f32[64,8,512]{2,1,0:T(8,128)} all-to-all(f32[64,8,512]{2,1,0:T(8,128)S(1)} %get-tuple-element.13), channel_id=1, replica_groups=mesh['seq'=64,'chan'=4] {'seq'}, dimensions={0} | all-to-all | bytes 2097152 | tf_op jit(solution)/shard_map/all_to_all | solution.py:120
  503.7 25.9 %all-to-all-done.12 = f32[64,8,512]{2,1,0:T(8,128)} async-done(((f32[64,8,512]{2,1,0:T(8,128)}), f32[64,8,512]{2,1,0:T(8,128)}, u32[]{:S(2)}, u32[]{:S(2)}) %all-to-all-start.12) | async-done | bytes 1048608 | tf_op jit(solution)/shard_map/all_to_all | solution.py:119
  534.5 34.3 %all_to_all.135 = f32[64,8,512]{2,1,0:T(8,128)S(1)} all-to-all(f32[64,8,512]{2,1,0:T(8,128)S(1)} %bitcast.136), channel_id=1, replica_groups=mesh['seq'=64,'chan'=4] {'seq'}, dimensions={0} | all-to-all | bytes 2097152 | tf_op jit(solution)/shard_map/all_to_all | solution.py:128
  570.0 7.4 %psum.7 = f32[512]{0:T(512)S(1)} all-reduce(f32[512]{0:T(512)S(1)} %get-tuple-element.5), channel_id=1, replica_groups=mesh['seq'=64,'chan'=4] {'chan'}, use_global_device_ids=true, to_apply=%region_1.2 | all-reduce | flops 512 | bytes 4096 | tf_op jit(solution)/shard_map/psum | solution.py:132
  (61 shorter events, 140.1 us)
Async XLA Ops:
  0.0 40.9 %all-to-all-start.4 = ((f32[64,8,512]{2,1,0:T(8,128)}), f32[64,8,512]{2,1,0:T(8,128)}, u32[]{:S(2)}, u32[]{:S(2)}) async-start(f32[64,8,512]{2,1,0:T(8,128)} %bitcast.137), calls=%async_computation.4 | async-start | bytes 2097152 | tf_op jit(solution)/shard_map/all_to_all | solution.py:61
  12.2 2.5 copy-start.6
  12.2 25.6 %copy-start = (f32[512,512]{1,0:T(8,128)S(1)}, f32[512,512]{1,0:T(8,128)}, u32[]{:S(2)}) copy-start(f32[512,512]{1,0:T(8,128)} %param.8) | copy-start | bytes 3145732
  12.2 25.6 %copy-start.1 = (f32[512,512]{1,0:T(8,128)S(1)}, f32[512,512]{1,0:T(8,128)}, u32[]{:S(2)}) copy-start(f32[512,512]{1,0:T(8,128)} %param.7) | copy-start | bytes 3145732
  12.2 25.6 %copy-start.2 = (f32[512,512]{1,0:T(8,128)S(1)}, f32[512,512]{1,0:T(8,128)}, u32[]{:S(2)}) copy-start(f32[512,512]{1,0:T(8,128)} %param.6) | copy-start | bytes 3145732
  14.6 23.3 %collective-permute-start = (f32[3,2,512]{2,1,0:T(2,128)S(1)}, f32[3,2,512]{2,1,0:T(2,128)S(1)}, u32[]{:S(2)}, u32[]{:S(2)}) collective-permute-start(f32[3,2,512]{2,1,0:T(2,128)S(1)} %slice.36), channel_id=1, source_target_pairs={{0,4},{4,8},{8,12},{12,16},{16,20},{20,24},{24,28},{28,32},{32,36}... | collective-permute-start | bytes 36872 | tf_op jit(solution)/shard_map/ppermute | solution.py:12
  40.9 36.6 %all-to-all-start = ((f32[64,8,512]{2,1,0:T(8,128)}), f32[64,8,512]{2,1,0:T(8,128)}, u32[]{:S(2)}, u32[]{:S(2)}) async-start(f32[64,8,512]{2,1,0:T(8,128)} %fusion.57), calls=%async_computation | async-start | bytes 2097152 | tf_op jit(solution)/shard_map/all_to_all | solution.py:60
  77.6 5.8 %copy-start.3 = (f32[64,8,512]{2,0,1:T(8,128)S(1)}, f32[64,8,512]{2,0,1:T(8,128)}, u32[]{:S(2)}) copy-start(f32[64,8,512]{2,0,1:T(8,128)} %convolution_negate_fusion) | copy-start | bytes 3145732
  89.9 34.6 %all-to-all-start.6 = ((f32[64,8,512]{2,1,0:T(8,128)}), f32[64,8,512]{2,1,0:T(8,128)}, u32[]{:S(2)}, u32[]{:S(2)}) async-start(f32[64,8,512]{2,1,0:T(8,128)} %copy.22), calls=%async_computation.6 | async-start | bytes 2097152 | tf_op jit(solution)/shard_map/all_to_all | solution.py:82
  124.5 34.6 %all-to-all-start.5 = ((f32[64,8,512]{2,1,0:T(8,128)}), f32[64,8,512]{2,1,0:T(8,128)}, u32[]{:S(2)}, u32[]{:S(2)}) async-start(f32[64,8,512]{2,1,0:T(8,128)} %copy.21), calls=%async_computation.5 | async-start | bytes 2097152 | tf_op jit(solution)/shard_map/all_to_all | solution.py:81
  159.0 34.7 %all-to-all-start.2 = ((f32[64,8,512]{2,1,0:T(8,128)}), f32[64,8,512]{2,1,0:T(8,128)}, u32[]{:S(2)}, u32[]{:S(2)}) async-start(f32[64,8,512]{2,1,0:T(8,128)} %copy.18), calls=%async_computation.2 | async-start | bytes 2097152 | tf_op jit(solution)/shard_map/all_to_all | solution.py:80
  193.8 34.6 %all-to-all-start.1 = ((f32[64,8,512]{2,1,0:T(8,128)}), f32[64,8,512]{2,1,0:T(8,128)}, u32[]{:S(2)}, u32[]{:S(2)}) async-start(f32[64,8,512]{2,1,0:T(8,128)} %copy.17), calls=%async_computation.1 | async-start | bytes 2097152 | tf_op jit(solution)/shard_map/all_to_all | solution.py:79
  228.3 34.7 %all-to-all-start.7 = ((f32[64,8,512]{2,1,0:T(8,128)}), f32[64,8,512]{2,1,0:T(8,128)}, u32[]{:S(2)}, u32[]{:S(2)}) async-start(f32[64,8,512]{2,1,0:T(8,128)} %fusion.5), calls=%async_computation.7 | async-start | bytes 2097152 | tf_op jit(solution)/shard_map/all_to_all | solution.py:89
  263.0 34.8 %all-to-all-start.9 = ((f32[64,8,512]{2,1,0:T(8,128)}), f32[64,8,512]{2,1,0:T(8,128)}, u32[]{:S(2)}, u32[]{:S(2)}) async-start(f32[64,8,512]{2,1,0:T(8,128)} %fusion.3), calls=%async_computation.9 | async-start | bytes 2097152 | tf_op jit(solution)/shard_map/all_to_all | solution.py:90
  297.8 34.7 %all-to-all-start.3 = ((f32[64,8,512]{2,1,0:T(8,128)}), f32[64,8,512]{2,1,0:T(8,128)}, u32[]{:S(2)}, u32[]{:S(2)}) async-start(f32[64,8,512]{2,1,0:T(8,128)} %fusion.6), calls=%async_computation.3 | async-start | bytes 2097152 | tf_op jit(solution)/shard_map/all_to_all | solution.py:87
  404.5 34.6 %all-to-all-start.10 = ((f32[64,8,512]{2,1,0:T(8,128)}), f32[64,8,512]{2,1,0:T(8,128)}, u32[]{:S(2)}, u32[]{:S(2)}) async-start(f32[64,8,512]{2,1,0:T(8,128)} %get-tuple-element.7), calls=%async_computation.10 | async-start | bytes 2097152 | tf_op jit(solution)/shard_map/all_to_all | solution.py:107
  439.1 7.0 %copy-start.8 = (f32[512,512]{1,0:T(8,128)S(1)}, f32[512,512]{1,0:T(8,128)}, u32[]{:S(2)}) copy-start(f32[512,512]{1,0:T(8,128)} %fusion.18) | copy-start | bytes 3145732
  446.1 7.3 %copy-start.5 = (f32[64,8,512]{2,1,0:T(8,128)S(1)}, f32[64,8,512]{2,1,0:T(8,128)}, u32[]{:S(2)}) copy-start(f32[64,8,512]{2,1,0:T(8,128)} %all_to_all.133) | copy-start | bytes 3145732
  494.8 34.8 %all-to-all-start.12 = ((f32[64,8,512]{2,1,0:T(8,128)}), f32[64,8,512]{2,1,0:T(8,128)}, u32[]{:S(2)}, u32[]{:S(2)}) async-start(f32[64,8,512]{2,1,0:T(8,128)} %get-tuple-element.14), calls=%async_computation.12 | async-start | bytes 2097152 | tf_op jit(solution)/shard_map/all_to_all | solution.py:119
  529.6 3.1 copy-start.4
  532.7 36.1 %copy-start.7 = (f32[512]{0:T(512)S(1)}, f32[512]{0:T(512)}, u32[]{:S(2)}) copy-start(f32[512]{0:T(512)} %param.11) | copy-start | bytes 6148
where the time goes:
time: 589 us; the launch traced here: 580 us
  waiting for transfers between devices  228 us (39%)
  blocking collectives  145 us (25%)
  matrix products  106 us (18%)
  starting transfers between devices  73.6 us (12%)
  local copies, waits for them, and re-layouts  15.5 us (3%)
  other arithmetic  12 us (2%)
    dot_general x18, matrix products, apply_table(): jnp.dot(table, values, precision=lax.Precision.HIGHEST, preferred_element...  106 us
    all_to_all x1, blocking collectives, per_device(): lax.all_to_all(spec_imag, 'seq', split_axis=0, concat_axis=0, tiled=True)  34.5 us
    all_to_all x1, blocking collectives, per_device(): lax.all_to_all(out_of_order(joint_imag), 'seq', split_axis=0, concat_axis...  34.3 us
    all_to_all x1, blocking collectives, per_device(): lax.all_to_all(turned_imag, 'seq', split_axis=0, concat_axis=0, tiled=True)  34.3 us
    all_to_all x1, blocking collectives, per_device(): lax.all_to_all(inverse_block, 'seq', split_axis=0, concat_axis=1, tiled=T...  34.3 us
    all_to_all x1, waiting for transfers between devices, per_device(): lax.all_to_all(filter_real, 'seq', split_axis=0, concat_axis=1, tiled=True)  25.9 us
    all_to_all x1, waiting for transfers between devices, per_device(): lax.all_to_all(turned_real, 'seq', split_axis=0, concat_axis=0, tiled=True)  25.9 us
    all_to_all x1, waiting for transfers between devices, per_device(): lax.all_to_all(filter_imag, 'seq', split_axis=0, concat_axis=1, tiled=True)  25.9 us
  transfers between devices with their start and end apart: 12, of which 12 were waited for; matrix products, arithmetic and copies ran while one was open for 15% of the time, Pallas kernels for 0%

commit v1 on v0

v1 whole, which is shorter than its diff:
```python
import functools
import math

import jax
import jax.numpy as jnp
import numpy as np
from jax import lax
from jax.experimental import pallas as pl
from jax.experimental.pallas import tpu as pltpu
from jax.sharding import PartitionSpec as P

LANE = 128
ROWS = 8


def dft8(values, sign):
    def add(a, b):
        if a is None:
            return b
        return a if b is None else a + b

    def sub(a, b):
        if b is None:
            return a
        return -b if a is None else a - b

    def cadd(x, y):
        return (add(x[0], y[0]), add(x[1], y[1]))

    def csub(x, y):
        return (sub(x[0], y[0]), sub(x[1], y[1]))

    def turn(x):
        re, im = x
        if sign > 0:
            return (None if im is None else -im, re)
        return (im, None if re is None else -re)

    def dft4(x):
        a, b = cadd(x[0], x[2]), csub(x[0], x[2])
        c, d = cadd(x[1], x[3]), turn(csub(x[1], x[3]))
        return [cadd(a, c), cadd(b, d), csub(a, c), csub(b, d)]

    even = dft4(values[0::2])
    odd = dft4(values[1::2])
    half = math.sqrt(0.5)
    out = [None] * 8
    for k in range(4):
        re, im = odd[k]
        if k == 0:
            turned = (re, im)
        elif k == 2:
            turned = turn((re, im))
        else:
            first = 1 if k == 1 else -1
            if im is None:
                turned = (first * half * re, sign * half * re)
            else:
                r = re if first > 0 else -re
                i = im if first > 0 else -im
                if sign > 0:
                    turned = (half * (r - im), half * (re + i))
                else:
                    turned = (half * (r + im), half * (i - re))
        out[k] = cadd(even[k], turned)
        out[k + 4] = csub(even[k], turned)
    return out


def cmul(x, y):
    return (x[0] * y[0] - x[1] * y[1], x[0] * y[1] + x[1] * y[0])


CLASSES = (
    [8 * v for v in range(5)]
    + [u + 8 * v for u in (1, 2, 3) for v in range(8)]
    + [4 + 8 * v for v in range(4)]
)
COUNT = len(CLASSES)
SPAN = COUNT * ROWS


def place(k):
    return CLASSES.index(k)


def tables(shards, width):
    total = shards * width
    where = np.arange(width)
    turns = (np.array(CLASSES)[:, None] * where[None, :]) % total
    angle = 2.0 * np.pi * turns / total
    twist = np.stack([np.cos(angle), np.sin(angle)]).astype(np.float32)
    quarter = width // 4
    inner = 2.0 * np.pi * np.arange(4)[:, None] * np.arange(quarter)[None, :] / width
    post = np.stack([np.cos(inner), np.sin(inner)]).astype(np.float32)
    turns = (np.arange(quarter)[:, None] * np.arange(quarter)[None, :]) % quarter
    angle = 2.0 * np.pi * turns / quarter
    c, s = np.cos(angle), np.sin(angle)
    forward = np.block([[c, -s], [s, c]])
    backward = np.block([[c, s], [-s, c]])

    def split(table):
        high = table.astype(np.float32).astype(jnp.bfloat16)
        low = (table - high.astype(np.float64)).astype(np.float32).astype(jnp.bfloat16)
        return np.stack([high, low])

    return twist[:, :, None, :], post[:, :, None, :], split(forward), split(backward)


def split_dot(values, table_ref):
    high = values.astype(jnp.bfloat16)
    low = (values - high.astype(jnp.float32)).astype(jnp.bfloat16)
    t_high, t_low = table_ref[0], table_ref[1]
    dot = functools.partial(jnp.dot, preferred_element_type=jnp.float32)
    return dot(high, t_high) + (dot(low, t_high) + dot(high, t_low))


def sections_forward(x_ref, mid_re, mid_im, stage):
    for lane in range(4):
        sl = slice(lane * LANE, (lane + 1) * LANE)
        for b in range(8):
            col = [(x_ref[8 * a + b, :, sl], None) for a in range(8)]
            out = dft8(col, -1)
            for u in range(5):
                re, im = out[u]
                if u and b:
                    w = (math.cos(2 * math.pi * b * u / 64), -math.sin(2 * math.pi * b * u / 64))
                    if im is None:
                        re, im = re * w[0], re * w[1]
                    else:
                        re, im = cmul((re, im), w)
                stage[0, u * 8 + b] = re
                if im is not None:
                    stage[1, u * 8 + b] = im
        for u in range(5):
            values = []
            for b in range(8):
                real_only = u == 0 or (u == 4 and b == 0)
                values.append(
                    (stage[0, u * 8 + b], None if real_only else stage[1, u * 8 + b])
                )
            out = dft8(values, -1)
            for v in range(8):
                if u + 8 * v in CLASSES:
                    at = place(u + 8 * v)
                    re, im = out[v]
                    mid_re[at, :, sl] = re
                    mid_im[at, :, sl] = jnp.zeros_like(re) if im is None else im


def quarters_forward(mid_re, mid_im, twist, post, spec):
    @pl.loop(0, COUNT)
    def _(at):
        z = []
        for h in range(4):
            sl = slice(h * LANE, (h + 1) * LANE)
            re, im = mid_re[at, :, sl], mid_im[at, :, sl]
            c, s = twist[0, at, :, sl], twist[1, at, :, sl]
            z.append((re * c + im * s, im * c - re * s))
        a = (z[0][0] + z[2][0], z[0][1] + z[2][1])
        b = (z[0][0] - z[2][0], z[0][1] - z[2][1])
        c = (z[1][0] + z[3][0], z[1][1] + z[3][1])
        d = (z[1][1] - z[3][1], z[3][0] - z[1][0])
        outs = [
            (a[0] + c[0], a[1] + c[1]),
            (b[0] + d[0], b[1] + d[1]),
            (a[0] - c[0], a[1] - c[1]),
            (b[0] - d[0], b[1] - d[1]),
        ]
        for q in range(4):
            re, im = outs[q]
            if q:
                c, s = post[0, q], post[1, q]
                re, im = re * c + im * s, im * c - re * s
            rows = pl.ds(pl.multiple_of(q * SPAN + at * ROWS, ROWS), ROWS)
            spec[rows, 0:LANE] = re
            spec[rows, LANE : 2 * LANE] = im


def quarters_backward(spec, mid_re, mid_im, twist, post):
    @pl.loop(0, COUNT)
    def _(at):
        z = []
        for q in range(4):
            rows = pl.ds(pl.multiple_of(q * SPAN + at * ROWS, ROWS), ROWS)
            re, im = spec[rows, 0:LANE], spec[rows, LANE : 2 * LANE]
            if q:
                c, s = post[0, q], post[1, q]
                re, im = re * c - im * s, im * c + re * s
            z.append((re, im))
        a = (z[0][0] + z[2][0], z[0][1] + z[2][1])
        b = (z[0][0] - z[2][0], z[0][1] - z[2][1])
        c = (z[1][0] + z[3][0], z[1][1] + z[3][1])
        d = (z[3][1] - z[1][1], z[1][0] - z[3][0])
        outs = [
            (a[0] + c[0], a[1] + c[1]),
            (b[0] + d[0], b[1] + d[1]),
            (a[0] - c[0], a[1] - c[1]),
            (b[0] - d[0], b[1] - d[1]),
        ]
        for h in range(4):
            sl = slice(h * LANE, (h + 1) * LANE)
            re, im = outs[h]
            c, s = twist[0, at, :, sl], twist[1, at, :, sl]
            mid_re[at, :, sl] = re * c - im * s
            mid_im[at, :, sl] = im * c + re * s


def sections_backward(mid_re, mid_im, y_ref, stage, scale):
    for lane in range(4):
        sl = slice(lane * LANE, (lane + 1) * LANE)
        for u in range(5):
            values = []
            for v in range(8):
                k = u + 8 * v
                if k in CLASSES:
                    at = place(k)
                    if k in (0, 32):
                        values.append((mid_re[at, :, sl], None))
                    else:
                        values.append((mid_re[at, :, sl], mid_im[at, :, sl]))
                elif u == 0:
                    re, im = values[8 - v]
                    values.append((re, -im))
                else:
                    at = place(64 - k)
                    values.append((mid_re[at, :, sl], -mid_im[at, :, sl]))
            out = dft8(values, 1)
            for b in range(8):
                re, im = out[b]
                w = (
                    scale * math.cos(2 * math.pi * b * u / 64),
                    scale * math.sin(2 * math.pi * b * u / 64),
                )
                if u == 0:
                    stage[0, b] = re * w[0]
                elif u == 4:
                    stage[0, 32 + b] = re * w[0] - im * w[1]
                else:
                    if b == 0:
                        re, im = re * w[0], im * w[0]
                    else:
                        re, im = cmul((re, im), w)
                    stage[0, u * 8 + b] = re
                    stage[1, u * 8 + b] = im
        for b in range(8):
            values = [(stage[0, b], None)]
            for u in (1, 2, 3):
                values.append((stage[0, u * 8 + b], stage[1, u * 8 + b]))
            values.append((stage[0, 32 + b], None))
            for u in (3, 2, 1):
                values.append((values[u][0], -values[u][1]))
            out = dft8(values, 1)
            for a in range(8):
                y_ref[8 * a + b, :, sl] = out[a][0]


CHUNK = 176


def spectrum_kernel(x_ref, twist, post, fwd, spec, mid_re, mid_im, stage):
    sections_forward(x_ref, mid_re, mid_im, stage)
    quarters_forward(mid_re, mid_im, twist, post, spec)

    @pl.loop(0, 4 * SPAN // CHUNK)
    def _(i):
        rows = pl.ds(pl.multiple_of(i * CHUNK, CHUNK), CHUNK)
        spec[rows, :] = split_dot(spec[rows, :], fwd)


def convolve_kernel(
    scale, x_ref, filt, twist, post, fwd, bwd, y_ref, mid_re, mid_im, stage, spec
):
    sections_forward(x_ref, mid_re, mid_im, stage)
    quarters_forward(mid_re, mid_im, twist, post, spec)

    @pl.loop(0, 4 * SPAN // CHUNK)
    def _(i):
        rows = pl.ds(pl.multiple_of(i * CHUNK, CHUNK), CHUNK)
        x = split_dot(spec[rows, :], fwd)
        f = filt[rows, :]
        re, im = cmul((x[:, :LANE], x[:, LANE:]), (f[:, :LANE], f[:, LANE:]))
        spec[rows, :] = split_dot(jnp.concatenate([re, im], axis=1), bwd)

    quarters_backward(spec, mid_re, mid_im, twist, post)
    sections_backward(mid_re, mid_im, y_ref, stage, scale)


def fft_scratch(width):
    return [
        pltpu.VMEM((COUNT, ROWS, width), jnp.float32),
        pltpu.VMEM((COUNT, ROWS, width), jnp.float32),
        pltpu.VMEM((2, 40, ROWS, LANE), jnp.float32),
    ]


VM = pl.BlockSpec(memory_space=pltpu.VMEM)
PARAMS = pltpu.CompilerParams(vmem_limit_bytes=40 * 1024 * 1024)


def filter_kernel(first_ref, filter_ref, skip_ref, out_ref):
    height, width = filter_ref.shape
    for p in range(0, height, LANE):
        for c in range(0, width, LANE):
            tile = filter_ref[p : p + LANE, c : c + LANE]
            if p == 0:
                row = lax.broadcasted_iota(jnp.int32, tile.shape, 0)
                direct = skip_ref[:, c : c + LANE] * first_ref[...]
                tile = tile + jnp.where(row == 0, direct, 0.0)
            out_ref[c : c + LANE, p : p + LANE] = tile.T


def short_filter(x_ref, halo, taps, p, c):
    tile = x_ref[p : p + LANE, c : c + LANE]
    if p == 0:
        before = jnp.concatenate([halo, tile[: LANE - 2]], axis=0)
        one = jnp.concatenate([halo[1:2], tile[: LANE - 1]], axis=0)
    else:
        before = x_ref[p - 2 : p + LANE - 2, c : c + LANE]
        one = x_ref[p - 1 : p + LANE - 1, c : c + LANE]
    return taps[0:1] * tile + taps[1:2] * one + taps[2:3] * before


def gate_kernel(key_ref, value_ref, halo_ref, taps_ref, out_ref):
    height, width = key_ref.shape
    for c in range(0, width, LANE):
        sl = slice(c, c + LANE)
        for p in range(0, height, LANE):
            k = short_filter(key_ref, halo_ref[1, :, sl], taps_ref[:, 1, sl], p, c)
            v = short_filter(value_ref, halo_ref[2, :, sl], taps_ref[:, 2, sl], p, c)
            out_ref[sl, p : p + LANE] = (k * v).T


def query_kernel(query_ref, halo_ref, taps_ref, out_ref):
    height, width = query_ref.shape
    for c in range(0, width, LANE):
        sl = slice(c, c + LANE)
        for p in range(0, height, LANE):
            q = short_filter(query_ref, halo_ref[0, :, sl], taps_ref[:, 0, sl], p, c)
            out_ref[sl, p : p + LANE] = q.T


def response_kernel(query_ref, conv_ref, response_ref, energy_ref):
    height, width = query_ref.shape
    total = jnp.zeros((ROWS, width), jnp.float32)
    for r in range(0, height, ROWS):
        value = query_ref[r : r + ROWS, :] * conv_ref[r : r + ROWS, :]
        response_ref[r : r + ROWS, :] = value
        total = total + value * value
    energy_ref[...] = jnp.broadcast_to(jnp.sum(total, axis=0, keepdims=True), energy_ref.shape)


def norm_kernel(channels, response_ref, energy_ref, other_ref, out_ref):
    height, width = response_ref.shape
    mean = (energy_ref[...] + other_ref[...]) / channels
    gain = 1.0 / jnp.sqrt(mean[0:1] + 1e-06)
    for p in range(0, width, LANE):
        for c in range(0, height, LANE):
            tile = response_ref[c : c + LANE, p : p + LANE] * gain[:, p : p + LANE]
            out_ref[p : p + LANE, c : c + LANE] = tile.T


def call(kernel, outs, *args, scratch=(), flops=10_000_000, moved=4_000_000):
    return pl.pallas_call(
        kernel,
        out_shape=outs,
        in_specs=[VM] * len(args),
        out_specs=jax.tree.map(lambda _: VM, outs),
        scratch_shapes=scratch,
        compiler_params=PARAMS,
        cost_estimate=pl.CostEstimate(flops=flops, bytes_accessed=moved, transcendentals=0),
    )(*args)


def exchange(values):
    return lax.all_to_all(values, "seq", split_axis=0, concat_axis=0, tiled=True)


def shifted(value, axis, steps):
    count = lax.axis_size(axis)
    return lax.ppermute(value, axis, [(i, (i + steps) % count) for i in range(count)])


def per_device(proj_query, proj_key, proj_value, long_filter, short_weight, skip_gain):
    height, width = proj_query.shape
    shards = lax.axis_size("seq")
    position = lax.axis_index("seq")
    twist, post, fwd, bwd = (jnp.asarray(t) for t in tables(shards, height))
    block = jax.ShapeDtypeStruct((width, height), jnp.float32)
    cube = jax.ShapeDtypeStruct((shards, ROWS, height), jnp.float32)

    first = jnp.where(position == 0, 1.0, 0.0).astype(jnp.float32)
    first = jnp.broadcast_to(first, (1, LANE))
    filter_t = call(filter_kernel, block, first, long_filter, skip_gain[None, :])
    filter_cols = exchange(filter_t.reshape(shards, ROWS, height))

    tail = jnp.stack([a[height - 2 :, :] for a in (proj_query, proj_key, proj_value)])
    halo = shifted(tail, "seq", 1)
    product_t = call(gate_kernel, block, proj_key, proj_value, halo, short_weight)
    signal_cols = exchange(product_t.reshape(shards, ROWS, height))
    query_t = call(query_kernel, block, proj_query, halo, short_weight)

    spectrum = call(
        spectrum_kernel,
        jax.ShapeDtypeStruct((4 * SPAN, 2 * LANE), jnp.float32),
        filter_cols, twist, post, fwd,
        scratch=fft_scratch(height),
        flops=1_000_000_000,
    )
    conv_cols = call(
        functools.partial(convolve_kernel, 1.0 / (shards * height)),
        cube,
        signal_cols, spectrum, twist, post, fwd, bwd,
        scratch=fft_scratch(height) + [pltpu.VMEM((4 * SPAN, 2 * LANE), jnp.float32)],
        flops=2_000_000_000,
    )
    conv = exchange(conv_cols).reshape(width, height)
    response, energy = call(
        response_kernel,
        (block, jax.ShapeDtypeStruct((ROWS, height), jnp.float32)),
        query_t, conv,
    )
    paired = energy + lax.ppermute(energy, "chan", [(0, 1), (1, 0), (2, 3), (3, 2)])
    other = lax.ppermute(paired, "chan", [(0, 2), (2, 0), (1, 3), (3, 1)])
    channels = width * lax.axis_size("chan")
    return call(
        functools.partial(norm_kernel, float(channels)),
        jax.ShapeDtypeStruct((height, width), jnp.float32),
        response, paired, other,
    )


def solution(mesh):
    return jax.shard_map(
        per_device,
        mesh=mesh,
        in_specs=(
            P("seq", "chan"),
            P("seq", "chan"),
            P("seq", "chan"),
            P("seq", "chan"),
            P(None, None, "chan"),
            P("chan"),
        ),
        out_specs=P("seq", "chan"),
        check_vma=False,
    )
```

time: 589 us -> 132 us (0.22); the launches traced: 580 us -> 132 us
  blocking collectives: 145 us -> 0 us
  waiting for transfers between devices: 228 us -> 86.6 us
  matrix products: 106 us -> 0 us
  starting transfers between devices: 73.6 us -> 26.5 us
  Pallas kernels: 0 us -> 14.3 us
  other arithmetic: 12 us -> 0.01 us
  local copies, waits for them, and re-layouts: 15.5 us -> 4.18 us
    all_to_all x11 -> x3, waiting for transfers between devices: 205 us -> 54.1 us  [exchange(): lax.all_to_all(values, 'seq', split_axis=0, concat_axis=0, tiled=True)]
    all_to_all x4 -> x0, blocking collectives: 137 us -> none  [the longest x1 34.5 us: per_device(): lax.all_to_all(spec_imag, 'seq', split_axis=0, concat_axis=0, tiled=True)]
    dot_general x18 -> x0, matrix products: 106 us -> none  [apply_table(): jnp.dot(table, values, precision=lax.Precision.HIGHEST, preferred_element...]
    all_to_all x11 -> x3, starting transfers between devices: 73.5 us -> 24.3 us  [exchange(): lax.all_to_all(values, 'seq', split_axis=0, concat_axis=0, tiled=True)]
    pallas_call x0 -> x7, Pallas kernels: none -> 14.3 us  [call(): pl.pallas_call(kernel, out_shape=outs, in_specs=[VM] * len(args), out_spe...]
    ppermute x1 -> x3, waiting for transfers between devices: 23.1 us -> 32.5 us  [the longest x1 25.5 us: shifted(): lax.ppermute(value, axis, [(i, (i + steps) % count) for i in range(count)])]
    psum x1 -> x0, blocking collectives: 7.45 us -> none  [per_device(): energy = lax.psum(jnp.sum(response * response, axis=1), 'chan')]
  transfers between devices with their start and end apart: 12 -> 6, of which waited for: 12 -> 6; matrix products, arithmetic and copies ran while one was open for 15% -> 0% of each run, Pallas kernels for 0% -> 4%
where the time goes in v1:
time: 132 us
  waiting for transfers between devices  86.6 us (66%)
  starting transfers between devices  26.5 us (20%)
  Pallas kernels  14.3 us (11%)
  local copies, waits for them, and re-layouts  4.18 us (3%)
    all_to_all x3, waiting for transfers between devices, exchange(): lax.all_to_all(values, 'seq', split_axis=0, concat_axis=0, tiled=True)  54.1 us
    ppermute x1, waiting for transfers between devices, shifted(): lax.ppermute(value, axis, [(i, (i + steps) % count) for i in range(count)])  25.5 us
    all_to_all x3, starting transfers between devices, exchange(): lax.all_to_all(values, 'seq', split_axis=0, concat_axis=0, tiled=True)  24.3 us
    pallas_call x7, Pallas kernels, call(): pl.pallas_call(kernel, out_shape=outs, in_specs=[VM] * len(args), out_spe...  14.3 us
    unnamed x24, local copies, waits for them, and re-layouts  4.17 us
    ppermute x1, waiting for transfers between devices, per_device(): other = lax.ppermute(paired, 'chan', [(0, 2), (2, 0), (1, 3), (3, 1)])  4.01 us
    ppermute x1, waiting for transfers between devices, per_device(): lax.ppermute(energy, 'chan', [(0, 1), (1, 0), (2, 3), (3, 2)])  3 us
  transfers between devices with their start and end apart: 6, of which 6 were waited for; matrix products, arithmetic and copies ran while one was open for 0% of the time, Pallas kernels for 4%

profile of v1, /device:TPU:24, one launch (start us, length us, event | category | flops | bytes accessed | tf_op | source)
XLA Modules:
  0.0 131.6 jit_solution(15792866208524101848)
XLA Ops:
  0.0 1.2 copy-done.3
  1.2 0.7 copy-done.5
  1.9 1.3 shard_map.102
  3.2 12.3 %all-to-all-start.1 = ((f32[64,8,512]{2,1,0:T(8,128)}), f32[64,8,512]{2,1,0:T(8,128)}, u32[]{:S(2)}, u32[]{:S(2)}) async-start(f32[64,8,512]{2,1,0:T(8,128)} %bitcast.5), calls=%async_computation.1 | async-start | bytes 2097152 | tf_op jit(solution)/shard_map/all_to_all | solution.py:376
  15.6 0.1 collective-permute-start
  15.7 25.5 %collective-permute-done.halo_ref = f32[3,2,512]{2,1,0:T(2,128)S(1)} collective-permute-done((f32[3,2,512]{2,1,0:T(2,128)S(1)}, f32[3,2,512]{2,1,0:T(2,128)S(1)}, u32[]{:S(2)}, u32[]{:S(2)}) %collective-permute-start) | collective-permute-done | bytes 12320 | tf_op jit(solution)/shard_map/ppermute | solution.py:381
  41.2 1.7 %shard_map.101 = f32[512,512]{1,0:T(8,128)} custom-call(f32[512,512]{1,0:T(8,128)S(1)} %copy-done.1, f32[512,512]{1,0:T(8,128)S(1)} %copy-done, f32[3,2,512]{2,1,0:T(2,128)S(1)} %collective-permute-done.halo_ref, f32[3,3,512]{2,1,0:T(4,128)S(1)} %copy-done.4), custom_call_target="tpu_custom_call" | custom-call | flops 10000000 | bytes 4000000 | tf_op jit(solution)/shard_map/pallas_call | solution.py:364
  42.9 1.4 %all-to-all-done.1.x_ref = f32[64,8,512]{2,1,0:T(8,128)} async-done(((f32[64,8,512]{2,1,0:T(8,128)}), f32[64,8,512]{2,1,0:T(8,128)}, u32[]{:S(2)}, u32[]{:S(2)}) %all-to-all-start.1) | async-done | bytes 1048608 | tf_op jit(solution)/shard_map/all_to_all | solution.py:376
  44.3 6.4 %all-to-all-start = ((f32[64,8,512]{2,1,0:T(8,128)}), f32[64,8,512]{2,1,0:T(8,128)S(1)}, u32[]{:S(2)}, u32[]{:S(2)}) async-start(f32[64,8,512]{2,1,0:T(8,128)} %bitcast.3), calls=%async_computation | async-start | bytes 2097152 | tf_op jit(solution)/shard_map/all_to_all | solution.py:376
  50.8 0.0 copy-start.7
  50.8 3.6 %shard_map.103.filt = f32[1056,256]{1,0:T(8,128)S(1)} custom-call(f32[64,8,512]{2,1,0:T(8,128)} %all-to-all-done.1.x_ref, f32[2,33,1,512]{3,2,1,0:T(1,128)S(1)} %copy-done.8, f32[2,4,1,128]{3,2,1,0:T(1,128)S(1)} %copy-done.9, bf16[2,256,256]{2,1,0:T(8,128)(2,1)S(1)} %copy-done.6), custom_call_target="tpu_custom_call" | custom-call | flops 1000000000 | bytes 4000000 | tf_op jit(solution)/shard_map/pallas_call | solution.py:364
  54.4 1.0 copy-done.10
  55.4 24.2 %all-to-all-done.x_ref = f32[64,8,512]{2,1,0:T(8,128)S(1)} async-done(((f32[64,8,512]{2,1,0:T(8,128)}), f32[64,8,512]{2,1,0:T(8,128)S(1)}, u32[]{:S(2)}, u32[]{:S(2)}) %all-to-all-start) | async-done | bytes 1048608 | tf_op jit(solution)/shard_map/all_to_all | solution.py:376
  79.6 1.2 copy-done.11
  80.9 5.8 %shard_map.104 = f32[64,8,512]{2,1,0:T(8,128)} custom-call(f32[64,8,512]{2,1,0:T(8,128)S(1)} %all-to-all-done.x_ref, f32[1056,256]{1,0:T(8,128)S(1)} %copy-done.11, f32[2,33,1,512]{3,2,1,0:T(1,128)S(1)} %copy-done.8, f32[2,4,1,128]{3,2,1,0:T(1,128)S(1)} %copy-done.9, bf16[2,256,256]{2,1,0:T(8,128)(2,1)S(1)} %copy-done.6, bf16[2,256,256]{2,1,0:T(8,128)(2,1)S(1)} %copy-done.7), custom_call_target="tpu_custom_call" | custom-call | flops 2000000000 | bytes 4000000 | tf_op jit(solution)/shard_map/pallas_call | solution.py:364
  86.7 5.6 %all-to-all-start.2 = ((f32[64,8,512]{2,1,0:T(8,128)}), f32[64,8,512]{2,1,0:T(8,128)S(1)}, u32[]{:S(2)}, u32[]{:S(2)}) async-start(f32[64,8,512]{2,1,0:T(8,128)} %shard_map.104), calls=%async_computation.2 | async-start | bytes 2097152 | tf_op jit(solution)/shard_map/all_to_all | solution.py:376
  92.2 0.4 shard_map.100.query_ref
  92.6 28.5 %all-to-all-done.2 = f32[64,8,512]{2,1,0:T(8,128)S(1)} async-done(((f32[64,8,512]{2,1,0:T(8,128)}), f32[64,8,512]{2,1,0:T(8,128)S(1)}, u32[]{:S(2)}, u32[]{:S(2)}) %all-to-all-start.2) | async-done | bytes 1048608 | tf_op jit(solution)/shard_map/all_to_all | solution.py:376
  121.1 0.1 shard_map.105
  121.2 0.8 collective-permute-start.1
  122.1 3.0 %collective-permute-done.1 = f32[8,512]{1,0:T(8,128)S(1)} collective-permute-done((f32[8,512]{1,0:T(8,128)S(1)}, f32[8,512]{1,0:T(8,128)S(1)}, u32[]{:S(2)}, u32[]{:S(2)}) %collective-permute-start.1) | collective-permute-done | bytes 16416 | tf_op jit(solution)/shard_map/ppermute | solution.py:423
  125.1 1.2 collective-permute-start.2
  126.3 4.0 %collective-permute-done.2.other_ref = f32[8,512]{1,0:T(8,128)S(1)} collective-permute-done((f32[8,512]{1,0:T(8,128)S(1)}, f32[8,512]{1,0:T(8,128)S(1)}, u32[]{:S(2)}, u32[]{:S(2)}) %collective-permute-start.2) | collective-permute-done | bytes 16416 | tf_op jit(solution)/shard_map/ppermute | solution.py:424
  130.3 1.3 %shard_map.106 = f32[512,512]{1,0:T(8,128)} custom-call(f32[512,512]{1,0:T(8,128)S(1)} %get-tuple-element.7.response_ref, f32[8,512]{1,0:T(8,128)S(1)} %add.3.energy_ref, f32[8,512]{1,0:T(8,128)S(1)} %collective-permute-done.2.other_ref), custom_call_target="tpu_custom_call" | custom-call | flops 10000000 | bytes 4000000 | tf_op jit(solution)/shard_map/pallas_call | solution.py:364
  (24 shorter events, 0.1 us)
Async XLA Ops:
  0.0 1.2 copy-start.3
  1.2 0.7 copy-start.5
  1.9 13.7 %copy-start.2 = (f32[512,512]{1,0:T(8,128)S(1)}, f32[512,512]{1,0:T(8,128)}, u32[]{:S(2)}) copy-start(f32[512,512]{1,0:T(8,128)} %query_ref.1) | copy-start | bytes 3145732
  3.2 12.4 %copy-start = (f32[512,512]{1,0:T(8,128)S(1)}, f32[512,512]{1,0:T(8,128)}, u32[]{:S(2)}) copy-start(f32[512,512]{1,0:T(8,128)} %value_ref.1) | copy-start | bytes 3145732
  3.2 12.4 %copy-start.1 = (f32[512,512]{1,0:T(8,128)S(1)}, f32[512,512]{1,0:T(8,128)}, u32[]{:S(2)}) copy-start(f32[512,512]{1,0:T(8,128)} %key_ref.1) | copy-start | bytes 3145732
  3.2 38.0 %copy-start.4 = (f32[3,3,512]{2,1,0:T(4,128)S(1)}, f32[3,3,512]{2,1,0:T(4,128)}, u32[]{:S(2)}) copy-start(f32[3,3,512]{2,1,0:T(4,128)} %taps_ref.3) | copy-start | bytes 55300
  3.2 41.1 %all-to-all-start.1 = ((f32[64,8,512]{2,1,0:T(8,128)}), f32[64,8,512]{2,1,0:T(8,128)}, u32[]{:S(2)}, u32[]{:S(2)}) async-start(f32[64,8,512]{2,1,0:T(8,128)} %bitcast.5), calls=%async_computation.1 | async-start | bytes 2097152 | tf_op jit(solution)/shard_map/all_to_all | solution.py:376
  15.6 25.6 %collective-permute-start = (f32[3,2,512]{2,1,0:T(2,128)S(1)}, f32[3,2,512]{2,1,0:T(2,128)S(1)}, u32[]{:S(2)}, u32[]{:S(2)}) collective-permute-start(f32[3,2,512]{2,1,0:T(2,128)S(1)} %pad_maximum_fusion), channel_id=1, source_target_pairs={{0,4},{4,8},{8,12},{12,16},{16,20},{20,24},{24,28},{28,32},{32,36}... | collective-permute-start | bytes 36872 | tf_op jit(solution)/shard_map/ppermute | solution.py:381
  42.9 7.8 %copy-start.6 = (bf16[2,256,256]{2,1,0:T(8,128)(2,1)S(1)}, bf16[2,256,256]{2,1,0:T(8,128)(2,1)}, u32[]{:S(2)}) copy-start(bf16[2,256,256]{2,1,0:T(8,128)(2,1)} %constant.22.clone.fwd) | copy-start | bytes 786436
  42.9 7.8 %copy-start.8 = (f32[2,33,1,512]{3,2,1,0:T(1,128)S(1)}, f32[2,33,1,512]{3,2,1,0:T(1,128)}, u32[]{:S(2)}) copy-start(f32[2,33,1,512]{3,2,1,0:T(1,128)} %constant.20.clone.twist) | copy-start | bytes 405508
  42.9 7.8 %copy-start.9 = (f32[2,4,1,128]{3,2,1,0:T(1,128)S(1)}, f32[2,4,1,128]{3,2,1,0:T(1,128)}, u32[]{:S(2)}) copy-start(f32[2,4,1,128]{3,2,1,0:T(1,128)} %constant.21.clone.post) | copy-start | bytes 12292
  44.3 35.3 %all-to-all-start = ((f32[64,8,512]{2,1,0:T(8,128)}), f32[64,8,512]{2,1,0:T(8,128)S(1)}, u32[]{:S(2)}, u32[]{:S(2)}) async-start(f32[64,8,512]{2,1,0:T(8,128)} %bitcast.3), calls=%async_computation | async-start | bytes 2097152 | tf_op jit(solution)/shard_map/all_to_all | solution.py:376
  50.8 28.9 %copy-start.7 = (bf16[2,256,256]{2,1,0:T(8,128)(2,1)S(1)}, bf16[2,256,256]{2,1,0:T(8,128)(2,1)}, u32[]{:S(2)}) copy-start(bf16[2,256,256]{2,1,0:T(8,128)(2,1)} %constant.23.clone.bwd) | copy-start | bytes 786436
  54.4 1.0 copy-start.10
  79.6 1.2 copy-start.11
  86.7 34.5 %all-to-all-start.2 = ((f32[64,8,512]{2,1,0:T(8,128)}), f32[64,8,512]{2,1,0:T(8,128)S(1)}, u32[]{:S(2)}, u32[]{:S(2)}) async-start(f32[64,8,512]{2,1,0:T(8,128)} %shard_map.104), calls=%async_computation.2 | async-start | bytes 2097152 | tf_op jit(solution)/shard_map/all_to_all | solution.py:376
  121.2 3.8 %collective-permute-start.1 = (f32[8,512]{1,0:T(8,128)S(1)}, f32[8,512]{1,0:T(8,128)S(1)}, u32[]{:S(2)}, u32[]{:S(2)}) collective-permute-start(f32[8,512]{1,0:T(8,128)S(1)} %get-tuple-element.8), channel_id=1, source_target_pairs={{0,1},{1,0},{2,3},{3,2},{4,5},{5,4},{6,7},{7,6},{8,9},{9,8},{10,11... | collective-permute-start | bytes 49160 | tf_op jit(solution)/shard_map/ppermute | solution.py:423
  125.1 5.2 %collective-permute-start.2 = (f32[8,512]{1,0:T(8,128)S(1)}, f32[8,512]{1,0:T(8,128)S(1)}, u32[]{:S(2)}, u32[]{:S(2)}) collective-permute-start(f32[8,512]{1,0:T(8,128)S(1)} %add.3.energy_ref), channel_id=1, source_target_pairs={{0,2},{2,0},{1,3},{3,1},{4,6},{6,4},{5,7},{7,5},{8,10},{10,8},{9,1... | collective-permute-start | bytes 49160 | tf_op jit(solution)/shard_map/ppermute | solution.py:424

commit v2 on v1

v2 whole, which is shorter than its diff:
```python
import functools
import math

import jax
import jax.numpy as jnp
import numpy as np
from jax import lax
from jax.experimental import pallas as pl
from jax.experimental.pallas import tpu as pltpu
from jax.sharding import PartitionSpec as P

LANE = 128
ROWS = 8


def dft8(values, sign):
    def add(a, b):
        if a is None:
            return b
        return a if b is None else a + b

    def sub(a, b):
        if b is None:
            return a
        return -b if a is None else a - b

    def cadd(x, y):
        return (add(x[0], y[0]), add(x[1], y[1]))

    def csub(x, y):
        return (sub(x[0], y[0]), sub(x[1], y[1]))

    def turn(x):
        re, im = x
        if sign > 0:
            return (None if im is None else -im, re)
        return (im, None if re is None else -re)

    def dft4(x):
        a, b = cadd(x[0], x[2]), csub(x[0], x[2])
        c, d = cadd(x[1], x[3]), turn(csub(x[1], x[3]))
        return [cadd(a, c), cadd(b, d), csub(a, c), csub(b, d)]

    even = dft4(values[0::2])
    odd = dft4(values[1::2])
    half = math.sqrt(0.5)
    out = [None] * 8
    for k in range(4):
        re, im = odd[k]
        if k == 0:
            turned = (re, im)
        elif k == 2:
            turned = turn((re, im))
        else:
            first = 1 if k == 1 else -1
            if im is None:
                turned = (first * half * re, sign * half * re)
            else:
                r = re if first > 0 else -re
                i = im if first > 0 else -im
                if sign > 0:
                    turned = (half * (r - im), half * (re + i))
                else:
                    turned = (half * (r + im), half * (i - re))
        out[k] = cadd(even[k], turned)
        out[k + 4] = csub(even[k], turned)
    return out


def cmul(x, y):
    return (x[0] * y[0] - x[1] * y[1], x[0] * y[1] + x[1] * y[0])


CLASSES = (
    [8 * v for v in range(5)]
    + [u + 8 * v for u in (1, 2, 3) for v in range(8)]
    + [4 + 8 * v for v in range(4)]
)
COUNT = len(CLASSES)
SPAN = COUNT * ROWS


def place(k):
    return CLASSES.index(k)


def tables(shards, width):
    total = shards * width
    where = np.arange(width)
    turns = (np.array(CLASSES)[:, None] * where[None, :]) % total
    angle = 2.0 * np.pi * turns / total
    twist = np.stack([np.cos(angle), np.sin(angle)]).astype(np.float32)
    quarter = width // 4
    inner = 2.0 * np.pi * np.arange(4)[:, None] * np.arange(quarter)[None, :] / width
    post = np.stack([np.cos(inner), np.sin(inner)]).astype(np.float32)
    turns = (np.arange(quarter)[:, None] * np.arange(quarter)[None, :]) % quarter
    angle = 2.0 * np.pi * turns / quarter
    c, s = np.cos(angle), np.sin(angle)
    forward = np.block([[c, -s], [s, c]])
    backward = np.block([[c, s], [-s, c]])

    def split(table):
        high = table.astype(np.float32).astype(jnp.bfloat16)
        low = (table - high.astype(np.float64)).astype(np.float32).astype(jnp.bfloat16)
        return np.stack([high, low])

    return twist[:, :, None, :], post[:, :, None, :], split(forward), split(backward)


def split_dot(values, table_ref):
    high = values.astype(jnp.bfloat16)
    low = (values - high.astype(jnp.float32)).astype(jnp.bfloat16)
    t_high, t_low = table_ref[0], table_ref[1]
    dot = functools.partial(jnp.dot, preferred_element_type=jnp.float32)
    return dot(high, t_high) + (dot(low, t_high) + dot(high, t_low))


UNROLL = 3


def over_classes(body):
    @pl.loop(0, COUNT // UNROLL)
    def _(i):
        for j in range(UNROLL):
            body(i * UNROLL + j)


def sections_forward(x_ref, mid_re, mid_im, stage, lane):
    sl = slice(lane * LANE, (lane + 1) * LANE)
    for b in range(8):
        col = [(x_ref[8 * a + b, :, sl], None) for a in range(8)]
        out = dft8(col, -1)
        for u in range(5):
            re, im = out[u]
            if u and b:
                w = (math.cos(2 * math.pi * b * u / 64), -math.sin(2 * math.pi * b * u / 64))
                if im is None:
                    re, im = re * w[0], re * w[1]
                else:
                    re, im = cmul((re, im), w)
            stage[0, u * 8 + b] = re
            if im is not None:
                stage[1, u * 8 + b] = im
    for u in range(5):
        values = []
        for b in range(8):
            real_only = u == 0 or (u == 4 and b == 0)
            values.append(
                (stage[0, u * 8 + b], None if real_only else stage[1, u * 8 + b])
            )
        out = dft8(values, -1)
        for v in range(8):
            if u + 8 * v in CLASSES:
                at = place(u + 8 * v)
                re, im = out[v]
                mid_re[at, :, sl] = re
                mid_im[at, :, sl] = jnp.zeros_like(re) if im is None else im


def quarters_forward(mid_re, mid_im, twist, post, spec):
    @over_classes
    def _(at):
        z = []
        for h in range(4):
            sl = slice(h * LANE, (h + 1) * LANE)
            re, im = mid_re[at, :, sl], mid_im[at, :, sl]
            c, s = twist[0, at, :, sl], twist[1, at, :, sl]
            z.append((re * c + im * s, im * c - re * s))
        a = (z[0][0] + z[2][0], z[0][1] + z[2][1])
        b = (z[0][0] - z[2][0], z[0][1] - z[2][1])
        c = (z[1][0] + z[3][0], z[1][1] + z[3][1])
        d = (z[1][1] - z[3][1], z[3][0] - z[1][0])
        outs = [
            (a[0] + c[0], a[1] + c[1]),
            (b[0] + d[0], b[1] + d[1]),
            (a[0] - c[0], a[1] - c[1]),
            (b[0] - d[0], b[1] - d[1]),
        ]
        for q in range(4):
            re, im = outs[q]
            if q:
                c, s = post[0, q], post[1, q]
                re, im = re * c + im * s, im * c - re * s
            rows = pl.ds(pl.multiple_of(q * SPAN + at * ROWS, ROWS), ROWS)
            spec[rows, 0:LANE] = re
            spec[rows, LANE : 2 * LANE] = im


def quarters_backward(spec, mid_re, mid_im, twist, post):
    @over_classes
    def _(at):
        z = []
        for q in range(4):
            rows = pl.ds(pl.multiple_of(q * SPAN + at * ROWS, ROWS), ROWS)
            re, im = spec[rows, 0:LANE], spec[rows, LANE : 2 * LANE]
            if q:
                c, s = post[0, q], post[1, q]
                re, im = re * c - im * s, im * c + re * s
            z.append((re, im))
        a = (z[0][0] + z[2][0], z[0][1] + z[2][1])
        b = (z[0][0] - z[2][0], z[0][1] - z[2][1])
        c = (z[1][0] + z[3][0], z[1][1] + z[3][1])
        d = (z[3][1] - z[1][1], z[1][0] - z[3][0])
        outs = [
            (a[0] + c[0], a[1] + c[1]),
            (b[0] + d[0], b[1] + d[1]),
            (a[0] - c[0], a[1] - c[1]),
            (b[0] - d[0], b[1] - d[1]),
        ]
        for h in range(4):
            sl = slice(h * LANE, (h + 1) * LANE)
            re, im = outs[h]
            c, s = twist[0, at, :, sl], twist[1, at, :, sl]
            mid_re[at, :, sl] = re * c - im * s
            mid_im[at, :, sl] = im * c + re * s


def sections_backward(mid_re, mid_im, y_ref, stage, scale, lane):
    sl = slice(lane * LANE, (lane + 1) * LANE)
    for u in range(5):
        values = []
        for v in range(8):
            k = u + 8 * v
            if k in CLASSES:
                at = place(k)
                if k in (0, 32):
                    values.append((mid_re[at, :, sl], None))
                else:
                    values.append((mid_re[at, :, sl], mid_im[at, :, sl]))
            elif u == 0:
                re, im = values[8 - v]
                values.append((re, -im))
            else:
                at = place(64 - k)
                values.append((mid_re[at, :, sl], -mid_im[at, :, sl]))
        out = dft8(values, 1)
        for b in range(8):
            re, im = out[b]
            w = (
                scale * math.cos(2 * math.pi * b * u / 64),
                scale * math.sin(2 * math.pi * b * u / 64),
            )
            if u == 0:
                stage[0, b] = re * w[0]
            elif u == 4:
                stage[0, 32 + b] = re * w[0] - im * w[1]
            else:
                if b == 0:
                    re, im = re * w[0], im * w[0]
                else:
                    re, im = cmul((re, im), w)
                stage[0, u * 8 + b] = re
                stage[1, u * 8 + b] = im
    for b in range(8):
        values = [(stage[0, b], None)]
        for u in (1, 2, 3):
            values.append((stage[0, u * 8 + b], stage[1, u * 8 + b]))
        values.append((stage[0, 32 + b], None))
        for u in (3, 2, 1):
            values.append((values[u][0], -values[u][1]))
        out = dft8(values, 1)
        for a in range(8):
            y_ref[8 * a + b, :, sl] = out[a][0]


def convolve_kernel(
    scale, cols, twist, post, fwd, bwd, out, inbox, y_ref, mid_re, mid_im, stage, filt, spec, got, sent
):
    loads = [
        [
            pltpu.make_async_copy(
                cols.at[:, pl.ds(part * ROWS, ROWS), pl.ds(lane * LANE, LANE)],
                inbox.at[part, :, :, pl.ds(lane * LANE, LANE)],
                got.at[part, lane],
            )
            for lane in range(4)
        ]
        for part in range(2)
    ]
    for part in range(2):
        for copy in loads[part]:
            copy.start()
    for part, into in ((0, filt), (1, spec)):
        for lane in range(4):
            loads[part][lane].wait()
            sections_forward(inbox.at[part], mid_re, mid_im, stage, lane)
        quarters_forward(mid_re, mid_im, twist, post, into)
        if part == 0:
            filt[...] = split_dot(filt[...], fwd)
    x = split_dot(spec[...], fwd)
    f = filt[...]
    re, im = cmul((x[:, :LANE], x[:, LANE:]), (f[:, :LANE], f[:, LANE:]))
    spec[...] = split_dot(jnp.concatenate([re, im], axis=1), bwd)
    quarters_backward(spec, mid_re, mid_im, twist, post)
    stores = []
    for lane in range(4):
        sections_backward(mid_re, mid_im, y_ref, stage, scale, lane)
        sl = pl.ds(lane * LANE, LANE)
        stores.append(pltpu.make_async_copy(y_ref.at[:, :, sl], out.at[:, :, sl], sent.at[lane]))
        stores[-1].start()
    for copy in stores:
        copy.wait()


VM = pl.BlockSpec(memory_space=pltpu.VMEM)
HB = pl.BlockSpec(memory_space=pltpu.HBM)
MIB = 1024 * 1024


def store_columns(out_ref, c, p, at, tile):
    turned = tile.T
    for g in range(tile.shape[1] // ROWS):
        out_ref[c // ROWS + g, at : at + ROWS, p : p + LANE] = turned[g * ROWS : (g + 1) * ROWS]


def short_filter(x_ref, halo, taps, p, c):
    tile = x_ref[p : p + LANE, c : c + LANE]
    if p == 0:
        before = jnp.concatenate([halo, tile[: LANE - 2]], axis=0)
        one = jnp.concatenate([halo[1:2], tile[: LANE - 1]], axis=0)
    else:
        before = x_ref[p - 2 : p + LANE - 2, c : c + LANE]
        one = x_ref[p - 1 : p + LANE - 1, c : c + LANE]
    return taps[0:1] * tile + taps[1:2] * one + taps[2:3] * before


def tail_kernel(query_ref, key_ref, value_ref, out_ref):
    for g, ref in enumerate((query_ref, key_ref, value_ref)):
        out_ref[g] = ref[ROWS - 2 :, :]


def columns_kernel(filter_ref, skip_ref, key_ref, value_ref, taps_ref, out_ref):
    height, width = key_ref.shape
    first = jnp.where(lax.axis_index("seq") == 0, 1.0, 0.0)
    for c in range(0, width, LANE):
        sl = slice(c, c + LANE)
        for p in range(0, height, LANE):
            tile = filter_ref[p : p + LANE, sl]
            if p == 0:
                row = lax.broadcasted_iota(jnp.int32, tile.shape, 0)
                tile = tile + jnp.where(row == 0, skip_ref[:, sl] * first, 0.0)
            store_columns(out_ref, c, p, 0, tile)
            if p:
                k = short_filter(key_ref, None, taps_ref[:, 1, sl], p, c)
                v = short_filter(value_ref, None, taps_ref[:, 2, sl], p, c)
                store_columns(out_ref, c, p, ROWS, k * v)


def edge_kernel(key_ref, value_ref, halo_ref, taps_ref, cols_ref, out_ref):
    del cols_ref
    width = key_ref.shape[1]
    for c in range(0, width, LANE):
        sl = slice(c, c + LANE)
        k = short_filter(key_ref, halo_ref[1, :, sl], taps_ref[:, 1, sl], 0, c)
        v = short_filter(value_ref, halo_ref[2, :, sl], taps_ref[:, 2, sl], 0, c)
        store_columns(out_ref, c, 0, ROWS, k * v)


def query_kernel(query_ref, halo_ref, taps_ref, out_ref):
    height, width = query_ref.shape
    for c in range(0, width, LANE):
        sl = slice(c, c + LANE)
        for p in range(0, height, LANE):
            q = short_filter(query_ref, halo_ref[0, :, sl], taps_ref[:, 0, sl], p, c)
            out_ref[sl, p : p + LANE] = q.T


def response_kernel(query_ref, conv_ref, response_ref, energy_ref):
    height, width = query_ref.shape
    total = jnp.zeros((ROWS, width), jnp.float32)
    for r in range(0, height, ROWS):
        value = query_ref[r : r + ROWS, :] * conv_ref[r : r + ROWS, :]
        response_ref[r : r + ROWS, :] = value
        total = total + value * value
    energy_ref[...] = jnp.broadcast_to(jnp.sum(total, axis=0, keepdims=True), energy_ref.shape)


def norm_kernel(channels, response_ref, energy_ref, e1, e2, e3, out_ref):
    height, width = response_ref.shape
    mean = (energy_ref[...] + e1[...] + e2[...] + e3[...]) / channels
    gain = 1.0 / jnp.sqrt(mean[0:1] + 1e-06)
    for p in range(0, width, LANE):
        for c in range(0, height, LANE):
            tile = response_ref[c : c + LANE, p : p + LANE] * gain[:, p : p + LANE]
            out_ref[p : p + LANE, c : c + LANE] = tile.T


def call(kernel, outs, *args, ins=None, out_specs=None, scratch=(), aliases=None, grid=(),
         vmem=16, flops=10_000_000, moved=4_000_000):
    return pl.pallas_call(
        kernel,
        out_shape=outs,
        grid=grid,
        in_specs=ins or [VM] * len(args),
        out_specs=out_specs or jax.tree.map(lambda _: VM, outs),
        scratch_shapes=scratch,
        input_output_aliases=aliases or {},
        compiler_params=pltpu.CompilerParams(vmem_limit_bytes=vmem * MIB),
        cost_estimate=pl.CostEstimate(flops=flops, bytes_accessed=moved, transcendentals=0),
    )(*args)


def exchange(values):
    return lax.all_to_all(values, "seq", split_axis=0, concat_axis=0, tiled=True)


def shifted(value, axis, steps):
    count = lax.axis_size(axis)
    return lax.ppermute(value, axis, [(i, (i + steps) % count) for i in range(count)])


def per_device(proj_query, proj_key, proj_value, long_filter, short_weight, skip_gain):
    height, width = proj_query.shape
    shards = lax.axis_size("seq")
    twist, post, fwd, bwd = (jnp.asarray(t) for t in tables(shards, height))
    block = jax.ShapeDtypeStruct((width, height), jnp.float32)
    pair = jax.ShapeDtypeStruct((shards, 2 * ROWS, height), jnp.float32)
    cube = jax.ShapeDtypeStruct((shards, ROWS, height), jnp.float32)

    last = pl.BlockSpec((ROWS, width), lambda i: (height // ROWS - 1, 0))
    tail = call(
        tail_kernel,
        jax.ShapeDtypeStruct((3, 2, width), jnp.float32),
        proj_query, proj_key, proj_value,
        grid=(1,),
        ins=[last] * 3,
        out_specs=pl.BlockSpec((3, 2, width), lambda i: (0, 0, 0)),
        moved=100_000,
    )
    halo = shifted(tail, "seq", 1)
    cols = call(
        columns_kernel, pair, long_filter, skip_gain[None, :], proj_key, proj_value, short_weight
    )
    cols = call(
        edge_kernel, pair, proj_key, proj_value, halo, short_weight, cols,
        ins=[VM, VM, VM, VM, VM],
        aliases={4: 0},
        moved=1_000_000,
    )
    cols = exchange(cols)
    query_t = call(query_kernel, block, proj_query, halo, short_weight)

    conv_cols = call(
        functools.partial(convolve_kernel, 1.0 / (shards * height)),
        cube,
        cols, twist, post, fwd, bwd,
        ins=[HB, VM, VM, VM, VM],
        out_specs=HB,
        scratch=[
            pltpu.VMEM((2, shards, ROWS, height), jnp.float32),
            pltpu.VMEM((shards, ROWS, height), jnp.float32),
            pltpu.VMEM((COUNT, ROWS, height), jnp.float32),
            pltpu.VMEM((COUNT, ROWS, height), jnp.float32),
            pltpu.VMEM((2, 40, ROWS, LANE), jnp.float32),
            pltpu.VMEM((4 * SPAN, 2 * LANE), jnp.float32),
            pltpu.VMEM((4 * SPAN, 2 * LANE), jnp.float32),
            pltpu.SemaphoreType.DMA((2, 4)),
            pltpu.SemaphoreType.DMA((4,)),
        ],
        flops=3_000_000_000,
        vmem=32,
    )
    conv = exchange(conv_cols).reshape(width, height)
    response, energy = call(
        response_kernel,
        (block, jax.ShapeDtypeStruct((ROWS, height), jnp.float32)),
        query_t, conv,
    )
    others = [shifted(energy, "chan", k) for k in (2, 1, 3)]
    channels = width * lax.axis_size("chan")
    return call(
        functools.partial(norm_kernel, float(channels)),
        jax.ShapeDtypeStruct((height, width), jnp.float32),
        response, energy, *others,
    )


def solution(mesh):
    return jax.shard_map(
        per_device,
        mesh=mesh,
        in_specs=(
            P("seq", "chan"),
            P("seq", "chan"),
            P("seq", "chan"),
            P("seq", "chan"),
            P(None, None, "chan"),
            P("chan"),
        ),
        out_specs=P("seq", "chan"),
        check_vma=False,
    )
```

time: 132 us -> 122 us (0.924)
  blocking collectives: 0 us -> 58.3 us
  waiting for transfers between devices: 86.6 us -> 39.2 us
  starting transfers between devices: 26.5 us -> 9.07 us
  Pallas kernels: 14.3 us -> 8.39 us
  local copies, waits for them, and re-layouts: 4.18 us -> 6.2 us
    all_to_all x0 -> x1, blocking collectives: none -> 58.3 us  [exchange(): lax.all_to_all(values, 'seq', split_axis=0, concat_axis=0, tiled=True)]
    all_to_all x3 -> x1, waiting for transfers between devices: 54.1 us -> 28.5 us  [exchange(): lax.all_to_all(values, 'seq', split_axis=0, concat_axis=0, tiled=True)]
    all_to_all x3 -> x1, starting transfers between devices: 24.3 us -> 5.48 us  [exchange(): lax.all_to_all(values, 'seq', split_axis=0, concat_axis=0, tiled=True)]
    ppermute x1 -> x4, waiting for transfers between devices: 25.5 us -> 10.7 us  [shifted(): lax.ppermute(value, axis, [(i, (i + steps) % count) for i in range(count)])]
    ppermute x2 -> x0, waiting for transfers between devices: 7.01 us -> none  [the longest x1 4.01 us: per_device(): other = lax.ppermute(paired, 'chan', [(0, 2), (2, 0), (1, 3), (3, 1)])]
    pallas_call x7, Pallas kernels: 14.3 us -> 8.39 us  [call(): pl.pallas_call(kernel, out_shape=outs, grid=grid, in_specs=ins or [VM] *...]
    ppermute x1 -> x4, starting transfers between devices: 0.08 us -> 3.59 us  [shifted(): lax.ppermute(value, axis, [(i, (i + steps) % count) for i in range(count)])]
    ppermute x2 -> x0, starting transfers between devices: 2.06 us -> none  [the longest x1 1.23 us: per_device(): other = lax.ppermute(paired, 'chan', [(0, 2), (2, 0), (1, 3), (3, 1)])]
  transfers between devices with their start and end apart: 6 -> 5, of which waited for: 6 -> 4; matrix products, arithmetic and copies ran while one was open for 0% -> 0% of each run, Pallas kernels for 4% -> 1%
where the time goes in v2:
time: 122 us; the launch traced here: 121 us
  blocking collectives  58.3 us (48%)
  waiting for transfers between devices  39.2 us (32%)
  starting transfers between devices  9.07 us (7%)
  Pallas kernels  8.39 us (7%)
  local copies, waits for them, and re-layouts  6.2 us (5%)
    all_to_all x1, blocking collectives, exchange(): lax.all_to_all(values, 'seq', split_axis=0, concat_axis=0, tiled=True)  58.3 us
    all_to_all x1, waiting for transfers between devices, exchange(): lax.all_to_all(values, 'seq', split_axis=0, concat_axis=0, tiled=True)  28.5 us
    ppermute x4, waiting for transfers between devices, shifted(): lax.ppermute(value, axis, [(i, (i + steps) % count) for i in range(count)])  10.7 us
    pallas_call x7, Pallas kernels, call(): pl.pallas_call(kernel, out_shape=outs, grid=grid, in_specs=ins or [VM] *...  8.39 us
    unnamed x28, local copies, waits for them, and re-layouts  6.2 us
    all_to_all x1, starting transfers between devices, exchange(): lax.all_to_all(values, 'seq', split_axis=0, concat_axis=0, tiled=True)  5.48 us
    ppermute x4, starting transfers between devices, shifted(): lax.ppermute(value, axis, [(i, (i + steps) % count) for i in range(count)])  3.59 us
  transfers between devices with their start and end apart: 5, of which 4 were waited for; matrix products, arithmetic and copies ran while one was open for 0% of the time, Pallas kernels for 1%

profile of v2, /device:TPU:24, one launch (start us, length us, event | category | flops | bytes accessed | tf_op | source)
XLA Modules:
  0.0 121.3 jit_solution(5807306039544536025)
XLA Ops:
  0.0 1.2 %copy-done = f32[512,512]{1,0:T(8,128)S(1)} copy-done((f32[512,512]{1,0:T(8,128)S(1)}, f32[512,512]{1,0:T(8,128)}, u32[]{:S(2)}) %copy-start) | copy-done | bytes 1048600
  1.2 1.2 %copy-done.2 = f32[512,512]{1,0:T(8,128)S(1)} copy-done((f32[512,512]{1,0:T(8,128)S(1)}, f32[512,512]{1,0:T(8,128)}, u32[]{:S(2)}) %copy-start.2) | copy-done | bytes 1048600
  2.5 1.2 %copy-done.4 = f32[512,512]{1,0:T(8,128)S(1)} copy-done((f32[512,512]{1,0:T(8,128)S(1)}, f32[512,512]{1,0:T(8,128)}, u32[]{:S(2)}) %copy-start.4) | copy-done | bytes 1048600
  3.7 0.1 collective-permute-start
  3.8 1.1 copy-done.1
  4.9 0.3 copy-done.3
  5.2 0.3 copy-done.6
  5.5 0.7 copy-done.7
  6.3 0.6 shard_map.102.cols_ref
  6.9 5.8 %collective-permute-done.halo_ref = f32[3,2,512]{2,1,0:T(2,128)S(1)} collective-permute-done((f32[3,2,512]{2,1,0:T(2,128)S(1)}, f32[3,2,512]{2,1,0:T(2,128)S(1)}, u32[]{:S(2)}, u32[]{:S(2)}) %collective-permute-start) | collective-permute-done | bytes 12320 | tf_op jit(solution)/shard_map/ppermute | solution.py:409
  12.7 0.2 shard_map.103
  12.9 0.0 copy-start.11
  12.9 0.0 copy-start.13
  12.9 58.3 %all_to_all.10.cols = f32[64,16,512]{2,1,0:T(8,128)S(1)} all-to-all(f32[64,16,512]{2,1,0:T(8,128)S(1)} %shard_map.103), channel_id=1, replica_groups=mesh['seq'=64,'chan'=4] {'seq'}, dimensions={0} | all-to-all | bytes 4194304 | tf_op jit(solution)/shard_map/all_to_all | solution.py:404
  71.3 5.7 %shard_map.104 = f32[64,8,512]{2,1,0:T(8,128)} custom-call(f32[64,16,512]{2,1,0:T(8,128)S(1)} %all_to_all.10.cols, f32[2,33,1,512]{3,2,1,0:T(1,128)S(1)} %copy-done.12, f32[2,4,1,128]{3,2,1,0:T(1,128)S(1)} %copy-done.13, bf16[2,256,256]{2,1,0:T(8,128)(2,1)S(1)} %copy-done.10, bf16[2,256,256]{2,1,0:T(8,128)(2,1)S(1)} %copy-done.11), custom_call_target="tpu_custom_call" | custom-call | flops 3000000000 | bytes 4000000 | tf_op jit(solution)/shard_map/pallas_call | solution.py:390
  77.1 5.5 %all-to-all-start.1 = ((f32[64,8,512]{2,1,0:T(8,128)}), f32[64,8,512]{2,1,0:T(8,128)S(1)}, u32[]{:S(2)}, u32[]{:S(2)}) async-start(f32[64,8,512]{2,1,0:T(8,128)} %shard_map.104), calls=%async_computation.1 | async-start | bytes 2097152 | tf_op jit(solution)/shard_map/all_to_all | solution.py:404
  82.6 0.4 shard_map.101.query_ref
  82.9 28.5 %all-to-all-done.1 = f32[64,8,512]{2,1,0:T(8,128)S(1)} async-done(((f32[64,8,512]{2,1,0:T(8,128)}), f32[64,8,512]{2,1,0:T(8,128)S(1)}, u32[]{:S(2)}, u32[]{:S(2)}) %all-to-all-start.1) | async-done | bytes 1048608 | tf_op jit(solution)/shard_map/all_to_all | solution.py:404
  111.4 0.1 shard_map.105
  111.6 1.3 %collective-permute-start.1 = (f32[8,512]{1,0:T(8,128)S(1)}, f32[8,512]{1,0:T(8,128)S(1)}, u32[]{:S(2)}, u32[]{:S(2)}) collective-permute-start(f32[8,512]{1,0:T(8,128)S(1)} %get-tuple-element.8.energy_ref), channel_id=1, source_target_pairs={{0,2},{1,3},{2,0},{3,1},{4,6},{5,7},{6,4},{7,5},{8,10},{9,11},{10,... | collective-permute-start | bytes 49160 | tf_op jit(solution)/shard_map/ppermute | solution.py:409
  112.9 2.2 %collective-permute-start.2 = (f32[8,512]{1,0:T(8,128)S(1)}, f32[8,512]{1,0:T(8,128)S(1)}, u32[]{:S(2)}, u32[]{:S(2)}) collective-permute-start(f32[8,512]{1,0:T(8,128)S(1)} %get-tuple-element.8.energy_ref), channel_id=1, source_target_pairs={{0,1},{1,2},{2,3},{3,0},{4,5},{5,6},{6,7},{7,4},{8,9},{9,10},{10,1... | collective-permute-start | bytes 49160 | tf_op jit(solution)/shard_map/ppermute | solution.py:409
  115.1 1.8 %collective-permute-done.1.e1 = f32[8,512]{1,0:T(8,128)S(1)} collective-permute-done((f32[8,512]{1,0:T(8,128)S(1)}, f32[8,512]{1,0:T(8,128)S(1)}, u32[]{:S(2)}, u32[]{:S(2)}) %collective-permute-start.1) | collective-permute-done | bytes 16416 | tf_op jit(solution)/shard_map/ppermute | solution.py:409
  116.9 3.1 %collective-permute-done.3.e3 = f32[8,512]{1,0:T(8,128)S(1)} collective-permute-done((f32[8,512]{1,0:T(8,128)S(1)}, f32[8,512]{1,0:T(8,128)S(1)}, u32[]{:S(2)}, u32[]{:S(2)}) %collective-permute-start.3) | collective-permute-done | bytes 16416 | tf_op jit(solution)/shard_map/ppermute | solution.py:409
  120.0 1.3 %shard_map.106 = f32[512,512]{1,0:T(8,128)} custom-call(f32[512,512]{1,0:T(8,128)S(1)} %get-tuple-element.7.response_ref, f32[8,512]{1,0:T(8,128)S(1)} %get-tuple-element.8.energy_ref, f32[8,512]{1,0:T(8,128)S(1)} %collective-permute-done.1.e1, f32[8,512]{1,0:T(8,128)S(1)} %collective-permute-done.2.e2, f32[8,512]{1,0:T(8,128)S(1)} %collective-permute-done.3.e3), custom_call_target="tpu_custom_call" | custom-call | flops 10000000 | bytes 4000000 | tf_op jit(solution)/shard_map/pallas_call | solution.py:390
  (22 shorter events, 0.1 us)
Async XLA Ops:
  0.0 1.2 %copy-start = (f32[512,512]{1,0:T(8,128)S(1)}, f32[512,512]{1,0:T(8,128)}, u32[]{:S(2)}) copy-start(f32[512,512]{1,0:T(8,128)} %key_ref.5) | copy-start | bytes 3145732
  1.2 1.2 %copy-start.2 = (f32[512,512]{1,0:T(8,128)S(1)}, f32[512,512]{1,0:T(8,128)}, u32[]{:S(2)}) copy-start(f32[512,512]{1,0:T(8,128)} %value_ref.5) | copy-start | bytes 3145732
  2.5 1.2 %copy-start.4 = (f32[512,512]{1,0:T(8,128)S(1)}, f32[512,512]{1,0:T(8,128)}, u32[]{:S(2)}) copy-start(f32[512,512]{1,0:T(8,128)} %query_ref.3) | copy-start | bytes 3145732
  3.7 1.2 %copy-start.1 = (f32[512,512]{1,0:T(8,128)S(1)}, f32[512,512]{1,0:T(8,128)}, u32[]{:S(2)}) copy-start(f32[512,512]{1,0:T(8,128)} %key_ref.5) | copy-start | bytes 3145732
  3.7 1.5 %copy-start.3 = (f32[512,512]{1,0:T(8,128)S(1)}, f32[512,512]{1,0:T(8,128)}, u32[]{:S(2)}) copy-start(f32[512,512]{1,0:T(8,128)} %value_ref.5) | copy-start | bytes 3145732
  3.7 1.9 %copy-start.6 = (f32[512,512]{1,0:T(8,128)S(1)}, f32[512,512]{1,0:T(8,128)}, u32[]{:S(2)}) copy-start(f32[512,512]{1,0:T(8,128)} %filter_ref.1) | copy-start | bytes 3145732
  3.7 1.9 %copy-start.9 = (f32[512]{0:T(512)S(1)}, f32[512]{0:T(512)}, u32[]{:S(2)}) copy-start(f32[512]{0:T(512)} %param.15) | copy-start | bytes 6148
  3.7 8.9 %collective-permute-start = (f32[3,2,512]{2,1,0:T(2,128)S(1)}, f32[3,2,512]{2,1,0:T(2,128)S(1)}, u32[]{:S(2)}, u32[]{:S(2)}) collective-permute-start(f32[3,2,512]{2,1,0:T(2,128)S(1)} %shard_map.100), channel_id=1, source_target_pairs={{0,4},{4,8},{8,12},{12,16},{16,20},{20,24},{24,28},{28,32},{32,36}... | collective-permute-start | bytes 36872 | tf_op jit(solution)/shard_map/ppermute | solution.py:409
  5.5 0.7 copy-start.7
  12.9 58.4 %copy-start.10 = (bf16[2,256,256]{2,1,0:T(8,128)(2,1)S(1)}, bf16[2,256,256]{2,1,0:T(8,128)(2,1)}, u32[]{:S(2)}) copy-start(bf16[2,256,256]{2,1,0:T(8,128)(2,1)} %constant.10.clone.fwd) | copy-start | bytes 786436
  12.9 58.4 %copy-start.11 = (bf16[2,256,256]{2,1,0:T(8,128)(2,1)S(1)}, bf16[2,256,256]{2,1,0:T(8,128)(2,1)}, u32[]{:S(2)}) copy-start(bf16[2,256,256]{2,1,0:T(8,128)(2,1)} %constant.11.clone.bwd) | copy-start | bytes 786436
  12.9 58.4 %copy-start.12 = (f32[2,33,1,512]{3,2,1,0:T(1,128)S(1)}, f32[2,33,1,512]{3,2,1,0:T(1,128)}, u32[]{:S(2)}) copy-start(f32[2,33,1,512]{3,2,1,0:T(1,128)} %constant.8.clone.twist) | copy-start | bytes 405508
  12.9 58.4 %copy-start.13 = (f32[2,4,1,128]{3,2,1,0:T(1,128)S(1)}, f32[2,4,1,128]{3,2,1,0:T(1,128)}, u32[]{:S(2)}) copy-start(f32[2,4,1,128]{3,2,1,0:T(1,128)} %constant.9.clone.post) | copy-start | bytes 12292
  77.0 5.5 %copy-start.5 = (f32[512,512]{1,0:T(8,128)S(1)}, f32[512,512]{1,0:T(8,128)}, u32[]{:S(2)}) copy-start(f32[512,512]{1,0:T(8,128)} %query_ref.3) | copy-start | bytes 3145732
  77.0 5.5 %copy-start.8 = (f32[3,3,512]{2,1,0:T(4,128)S(1)}, f32[3,3,512]{2,1,0:T(4,128)}, u32[]{:S(2)}) copy-start(f32[3,3,512]{2,1,0:T(4,128)} %taps_ref.5) | copy-start | bytes 55300
  77.1 34.4 %all-to-all-start.1 = ((f32[64,8,512]{2,1,0:T(8,128)}), f32[64,8,512]{2,1,0:T(8,128)S(1)}, u32[]{:S(2)}, u32[]{:S(2)}) async-start(f32[64,8,512]{2,1,0:T(8,128)} %shard_map.104), calls=%async_computation.1 | async-start | bytes 2097152 | tf_op jit(solution)/shard_map/all_to_all | solution.py:404
  111.6 5.3 %collective-permute-start.1 = (f32[8,512]{1,0:T(8,128)S(1)}, f32[8,512]{1,0:T(8,128)S(1)}, u32[]{:S(2)}, u32[]{:S(2)}) collective-permute-start(f32[8,512]{1,0:T(8,128)S(1)} %get-tuple-element.8.energy_ref), channel_id=1, source_target_pairs={{0,2},{1,3},{2,0},{3,1},{4,6},{5,7},{6,4},{7,5},{8,10},{9,11},{10,... | collective-permute-start | bytes 49160 | tf_op jit(solution)/shard_map/ppermute | solution.py:409
  112.9 4.0 %collective-permute-start.2 = (f32[8,512]{1,0:T(8,128)S(1)}, f32[8,512]{1,0:T(8,128)S(1)}, u32[]{:S(2)}, u32[]{:S(2)}) collective-permute-start(f32[8,512]{1,0:T(8,128)S(1)} %get-tuple-element.8.energy_ref), channel_id=1, source_target_pairs={{0,1},{1,2},{2,3},{3,0},{4,5},{5,6},{6,7},{7,4},{8,9},{9,10},{10,1... | collective-permute-start | bytes 49160 | tf_op jit(solution)/shard_map/ppermute | solution.py:409
  115.1 4.9 %collective-permute-start.3 = (f32[8,512]{1,0:T(8,128)S(1)}, f32[8,512]{1,0:T(8,128)S(1)}, u32[]{:S(2)}, u32[]{:S(2)}) collective-permute-start(f32[8,512]{1,0:T(8,128)S(1)} %get-tuple-element.8.energy_ref), channel_id=1, source_target_pairs={{0,3},{1,0},{2,1},{3,2},{4,7},{5,4},{6,5},{7,6},{8,11},{9,8},{10,9... | collective-permute-start | bytes 49160 | tf_op jit(solution)/shard_map/ppermute | solution.py:409

commit v3 on v2

--- a/solution.py
+++ b/solution.py
@@ -102,7 +102,7 @@
     def split(table):
         high = table.astype(np.float32).astype(jnp.bfloat16)
         low = (table - high.astype(np.float64)).astype(np.float32).astype(jnp.bfloat16)
-        return np.stack([high, low])
+        return np.concatenate([high, high, low])
 
     return twist[:, :, None, :], post[:, :, None, :], split(forward), split(backward)
 
@@ -110,12 +110,11 @@
 def split_dot(values, table_ref):
     high = values.astype(jnp.bfloat16)
     low = (values - high.astype(jnp.float32)).astype(jnp.bfloat16)
-    t_high, t_low = table_ref[0], table_ref[1]
-    dot = functools.partial(jnp.dot, preferred_element_type=jnp.float32)
-    return dot(high, t_high) + (dot(low, t_high) + dot(high, t_low))
-
-
-UNROLL = 3
+    parts = jnp.concatenate([high, low, high], axis=1)
+    return jnp.dot(parts, table_ref[...], preferred_element_type=jnp.float32)
+
+
+UNROLL = 33
 
 
 def over_classes(body):
@@ -125,10 +124,10 @@
             body(i * UNROLL + j)
 
 
-def sections_forward(x_ref, mid_re, mid_im, stage, lane):
+def sections_forward(x_ref, at, mid_re, mid_im, stage, lane):
     sl = slice(lane * LANE, (lane + 1) * LANE)
     for b in range(8):
-        col = [(x_ref[8 * a + b, :, sl], None) for a in range(8)]
+        col = [(x_ref[8 * a + b, at : at + ROWS, sl], None) for a in range(8)]
         out = dft8(col, -1)
         for u in range(5):
             re, im = out[u]
@@ -151,10 +150,10 @@
         out = dft8(values, -1)
         for v in range(8):
             if u + 8 * v in CLASSES:
-                at = place(u + 8 * v)
+                k = place(u + 8 * v)
                 re, im = out[v]
-                mid_re[at, :, sl] = re
-                mid_im[at, :, sl] = jnp.zeros_like(re) if im is None else im
+                mid_re[k, :, sl] = re
+                mid_im[k, :, sl] = jnp.zeros_like(re) if im is None else im
 
 
 def quarters_forward(mid_re, mid_im, twist, post, spec):
@@ -264,26 +263,11 @@
 
 
 def convolve_kernel(
-    scale, cols, twist, post, fwd, bwd, out, inbox, y_ref, mid_re, mid_im, stage, filt, spec, got, sent
+    scale, cols, twist, post, fwd, bwd, y_ref, mid_re, mid_im, stage, filt, spec
 ):
-    loads = [
-        [
-            pltpu.make_async_copy(
-                cols.at[:, pl.ds(part * ROWS, ROWS), pl.ds(lane * LANE, LANE)],
-                inbox.at[part, :, :, pl.ds(lane * LANE, LANE)],
-                got.at[part, lane],
-            )
-            for lane in range(4)
-        ]
-        for part in range(2)
-    ]
-    for part in range(2):
-        for copy in loads[part]:
-            copy.start()
     for part, into in ((0, filt), (1, spec)):
         for lane in range(4):
-            loads[part][lane].wait()
-            sections_forward(inbox.at[part], mid_re, mid_im, stage, lane)
+            sections_forward(cols, part * ROWS, mid_re, mid_im, stage, lane)
         quarters_forward(mid_re, mid_im, twist, post, into)
         if part == 0:
             filt[...] = split_dot(filt[...], fwd)
@@ -292,14 +276,8 @@
     re, im = cmul((x[:, :LANE], x[:, LANE:]), (f[:, :LANE], f[:, LANE:]))
     spec[...] = split_dot(jnp.concatenate([re, im], axis=1), bwd)
     quarters_backward(spec, mid_re, mid_im, twist, post)
-    stores = []
     for lane in range(4):
         sections_backward(mid_re, mid_im, y_ref, stage, scale, lane)
-        sl = pl.ds(lane * LANE, LANE)
-        stores.append(pltpu.make_async_copy(y_ref.at[:, :, sl], out.at[:, :, sl], sent.at[lane]))
-        stores[-1].start()
-    for copy in stores:
-        copy.wait()
 
 
 VM = pl.BlockSpec(memory_space=pltpu.VMEM)
@@ -329,7 +307,7 @@
         out_ref[g] = ref[ROWS - 2 :, :]
 
 
-def columns_kernel(filter_ref, skip_ref, key_ref, value_ref, taps_ref, out_ref):
+def columns_kernel(filter_ref, key_ref, value_ref, taps_ref, out_ref):
     height, width = key_ref.shape
     first = jnp.where(lax.axis_index("seq") == 0, 1.0, 0.0)
     for c in range(0, width, LANE):
@@ -338,7 +316,7 @@
             tile = filter_ref[p : p + LANE, sl]
             if p == 0:
                 row = lax.broadcasted_iota(jnp.int32, tile.shape, 0)
-                tile = tile + jnp.where(row == 0, skip_ref[:, sl] * first, 0.0)
+                tile = tile + jnp.where(row == 0, taps_ref[3, 0:1, sl] * first, 0.0)
             store_columns(out_ref, c, p, 0, tile)
             if p:
                 k = short_filter(key_ref, None, taps_ref[:, 1, sl], p, c)
@@ -375,14 +353,20 @@
     energy_ref[...] = jnp.broadcast_to(jnp.sum(total, axis=0, keepdims=True), energy_ref.shape)
 
 
-def norm_kernel(channels, response_ref, energy_ref, e1, e2, e3, out_ref):
+def norm_kernel(channels, response_ref, energy_ref, e1, e2, e3, out_ref, box, sems):
     height, width = response_ref.shape
     mean = (energy_ref[...] + e1[...] + e2[...] + e3[...]) / channels
     gain = 1.0 / jnp.sqrt(mean[0:1] + 1e-06)
-    for p in range(0, width, LANE):
+    copies = []
+    for i, p in enumerate(range(0, width, LANE)):
         for c in range(0, height, LANE):
             tile = response_ref[c : c + LANE, p : p + LANE] * gain[:, p : p + LANE]
-            out_ref[p : p + LANE, c : c + LANE] = tile.T
+            box[p : p + LANE, c : c + LANE] = tile.T
+        rows = pl.ds(p, LANE)
+        copies.append(pltpu.make_async_copy(box.at[rows], out_ref.at[rows], sems.at[i]))
+        copies[-1].start()
+    for copy in copies:
+        copy.wait()
 
 
 def call(kernel, outs, *args, ins=None, out_specs=None, scratch=(), aliases=None, grid=(),
@@ -417,48 +401,43 @@
     pair = jax.ShapeDtypeStruct((shards, 2 * ROWS, height), jnp.float32)
     cube = jax.ShapeDtypeStruct((shards, ROWS, height), jnp.float32)
 
+    direct = jnp.broadcast_to(skip_gain, (1, 3, width))
+    taps = jnp.concatenate([short_weight, direct])
     last = pl.BlockSpec((ROWS, width), lambda i: (height // ROWS - 1, 0))
     tail = call(
         tail_kernel,
         jax.ShapeDtypeStruct((3, 2, width), jnp.float32),
-        proj_query, proj_key, proj_value,
+        proj_query[height - ROWS :, :], proj_key, proj_value,
         grid=(1,),
-        ins=[last] * 3,
+        ins=[pl.BlockSpec((ROWS, width), lambda i: (0, 0)), last, last],
         out_specs=pl.BlockSpec((3, 2, width), lambda i: (0, 0, 0)),
         moved=100_000,
     )
     halo = shifted(tail, "seq", 1)
     cols = call(
-        columns_kernel, pair, long_filter, skip_gain[None, :], proj_key, proj_value, short_weight
+        columns_kernel, pair, long_filter, proj_key, proj_value, taps
     )
     cols = call(
-        edge_kernel, pair, proj_key, proj_value, halo, short_weight, cols,
-        ins=[VM, VM, VM, VM, VM],
+        edge_kernel, pair, proj_key, proj_value, halo, taps, cols,
         aliases={4: 0},
         moved=1_000_000,
     )
     cols = exchange(cols)
-    query_t = call(query_kernel, block, proj_query, halo, short_weight)
+    query_t = call(query_kernel, block, proj_query, halo, taps)
 
     conv_cols = call(
         functools.partial(convolve_kernel, 1.0 / (shards * height)),
         cube,
         cols, twist, post, fwd, bwd,
-        ins=[HB, VM, VM, VM, VM],
-        out_specs=HB,
         scratch=[
-            pltpu.VMEM((2, shards, ROWS, height), jnp.float32),
-            pltpu.VMEM((shards, ROWS, height), jnp.float32),
             pltpu.VMEM((COUNT, ROWS, height), jnp.float32),
             pltpu.VMEM((COUNT, ROWS, height), jnp.float32),
             pltpu.VMEM((2, 40, ROWS, LANE), jnp.float32),
             pltpu.VMEM((4 * SPAN, 2 * LANE), jnp.float32),
             pltpu.VMEM((4 * SPAN, 2 * LANE), jnp.float32),
-            pltpu.SemaphoreType.DMA((2, 4)),
-            pltpu.SemaphoreType.DMA((4,)),
         ],
         flops=3_000_000_000,
-        vmem=32,
+        vmem=24,
     )
     conv = exchange(conv_cols).reshape(width, height)
     response, energy = call(
@@ -472,6 +451,11 @@
         functools.partial(norm_kernel, float(channels)),
         jax.ShapeDtypeStruct((height, width), jnp.float32),
         response, energy, *others,
+        out_specs=HB,
+        scratch=[
+            pltpu.VMEM((height, width), jnp.float32),
+            pltpu.SemaphoreType.DMA((height // LANE,)),
+        ],
     )
 
 

time: 122 us -> 120 us (0.984)
    unnamed x28 -> x24, local copies, waits for them, and re-layouts: 6.2 us -> 5.1 us
where the time goes in v3:
time: 120 us
  blocking collectives  58.3 us (49%)
  waiting for transfers between devices  39.1 us (33%)
  starting transfers between devices  9.06 us (8%)
  Pallas kernels  7.3 us (6%)
  local copies, waits for them, and re-layouts  5.84 us (5%)
    all_to_all x1, blocking collectives, exchange(): lax.all_to_all(values, 'seq', split_axis=0, concat_axis=0, tiled=True)  58.3 us
    all_to_all x1, waiting for transfers between devices, exchange(): lax.all_to_all(values, 'seq', split_axis=0, concat_axis=0, tiled=True)  28.5 us
    ppermute x4, waiting for transfers between devices, shifted(): lax.ppermute(value, axis, [(i, (i + steps) % count) for i in range(count)])  10.6 us
    pallas_call x7, Pallas kernels, call(): pl.pallas_call(kernel, out_shape=outs, grid=grid, in_specs=ins or [VM] *...  7.3 us
    all_to_all x1, starting transfers between devices, exchange(): lax.all_to_all(values, 'seq', split_axis=0, concat_axis=0, tiled=True)  5.47 us
    unnamed x24, local copies, waits for them, and re-layouts  5.1 us
    ppermute x4, starting transfers between devices, shifted(): lax.ppermute(value, axis, [(i, (i + steps) % count) for i in range(count)])  3.59 us
  transfers between devices with their start and end apart: 5, of which 4 were waited for; matrix products, arithmetic and copies ran while one was open for 0% of the time, Pallas kernels for 1%

profile of v3, /device:TPU:24, one launch (start us, length us, event | category | flops | bytes accessed | tf_op | source)
XLA Modules:
  0.0 119.7 jit_solution(13680311442362407762)
XLA Ops:
  0.0 0.7 slice.3.query_ref
  0.7 1.2 %copy-done = f32[512,512]{1,0:T(8,128)S(1)} copy-done((f32[512,512]{1,0:T(8,128)S(1)}, f32[512,512]{1,0:T(8,128)}, u32[]{:S(2)}) %copy-start) | copy-done | bytes 1048600
  2.0 1.2 %copy-done.2 = f32[512,512]{1,0:T(8,128)S(1)} copy-done((f32[512,512]{1,0:T(8,128)S(1)}, f32[512,512]{1,0:T(8,128)}, u32[]{:S(2)}) %copy-start.2) | copy-done | bytes 1048600
  3.2 0.1 collective-permute-start
  3.3 1.1 copy-done.1
  4.4 0.3 copy-done.3
  4.7 1.2 %copy-done.5 = f32[512,512]{1,0:T(8,128)S(1)} copy-done((f32[512,512]{1,0:T(8,128)S(1)}, f32[512,512]{1,0:T(8,128)}, u32[]{:S(2)}) %copy-start.5) | copy-done | bytes 1048600
  6.0 0.6 shard_map.102.cols_ref
  6.5 5.6 %collective-permute-done.halo_ref = f32[3,2,512]{2,1,0:T(2,128)S(1)} collective-permute-done((f32[3,2,512]{2,1,0:T(2,128)S(1)}, f32[3,2,512]{2,1,0:T(2,128)S(1)}, u32[]{:S(2)}, u32[]{:S(2)}) %collective-permute-start) | collective-permute-done | bytes 12320 | tf_op jit(solution)/shard_map/ppermute | solution.py:393
  12.2 0.2 shard_map.103
  12.4 0.0 copy-start.7
  12.4 0.0 copy-start.8
  12.4 0.0 copy-start.9
  12.4 58.3 %all_to_all.10.cols = f32[64,16,512]{2,1,0:T(8,128)S(1)} all-to-all(f32[64,16,512]{2,1,0:T(8,128)S(1)} %shard_map.103), channel_id=1, replica_groups=mesh['seq'=64,'chan'=4] {'seq'}, dimensions={0} | all-to-all | bytes 4194304 | tf_op jit(solution)/shard_map/all_to_all | solution.py:388
  70.8 4.8 %shard_map.104 = f32[64,8,512]{2,1,0:T(8,128)} custom-call(f32[64,16,512]{2,1,0:T(8,128)S(1)} %all_to_all.10.cols, f32[2,33,1,512]{3,2,1,0:T(1,128)S(1)} %copy-done.8, f32[2,4,1,128]{3,2,1,0:T(1,128)S(1)} %copy-done.9, bf16[768,256]{1,0:T(8,128)(2,1)S(1)} %copy-done.6, bf16[768,256]{1,0:T(8,128)(2,1)S(1)} %copy-done.7), custom_call_target="tpu_custom_call" | custom-call | flops 3000000000 | bytes 4000000 | tf_op jit(solution)/shard_map/pallas_call | solution.py:374
  75.6 5.5 %all-to-all-start.1 = ((f32[64,8,512]{2,1,0:T(8,128)}), f32[64,8,512]{2,1,0:T(8,128)S(1)}, u32[]{:S(2)}, u32[]{:S(2)}) async-start(f32[64,8,512]{2,1,0:T(8,128)} %shard_map.104), calls=%async_computation.1 | async-start | bytes 2097152 | tf_op jit(solution)/shard_map/all_to_all | solution.py:388
  81.1 0.4 shard_map.101.query_ref
  81.5 28.5 %all-to-all-done.1 = f32[64,8,512]{2,1,0:T(8,128)S(1)} async-done(((f32[64,8,512]{2,1,0:T(8,128)}), f32[64,8,512]{2,1,0:T(8,128)S(1)}, u32[]{:S(2)}, u32[]{:S(2)}) %all-to-all-start.1) | async-done | bytes 1048608 | tf_op jit(solution)/shard_map/all_to_all | solution.py:388
  110.0 0.1 shard_map.105
  110.1 1.3 %collective-permute-start.1 = (f32[8,512]{1,0:T(8,128)S(1)}, f32[8,512]{1,0:T(8,128)S(1)}, u32[]{:S(2)}, u32[]{:S(2)}) collective-permute-start(f32[8,512]{1,0:T(8,128)S(1)} %get-tuple-element.8.energy_ref), channel_id=1, source_target_pairs={{0,2},{1,3},{2,0},{3,1},{4,6},{5,7},{6,4},{7,5},{8,10},{9,11},{10,... | collective-permute-start | bytes 49160 | tf_op jit(solution)/shard_map/ppermute | solution.py:393
  111.4 2.2 %collective-permute-start.2 = (f32[8,512]{1,0:T(8,128)S(1)}, f32[8,512]{1,0:T(8,128)S(1)}, u32[]{:S(2)}, u32[]{:S(2)}) collective-permute-start(f32[8,512]{1,0:T(8,128)S(1)} %get-tuple-element.8.energy_ref), channel_id=1, source_target_pairs={{0,1},{1,2},{2,3},{3,0},{4,5},{5,6},{6,7},{7,4},{8,9},{9,10},{10,1... | collective-permute-start | bytes 49160 | tf_op jit(solution)/shard_map/ppermute | solution.py:393
  113.6 1.8 %collective-permute-done.1.e1 = f32[8,512]{1,0:T(8,128)S(1)} collective-permute-done((f32[8,512]{1,0:T(8,128)S(1)}, f32[8,512]{1,0:T(8,128)S(1)}, u32[]{:S(2)}, u32[]{:S(2)}) %collective-permute-start.1) | collective-permute-done | bytes 16416 | tf_op jit(solution)/shard_map/ppermute | solution.py:393
  115.4 3.1 %collective-permute-done.3.e3 = f32[8,512]{1,0:T(8,128)S(1)} collective-permute-done((f32[8,512]{1,0:T(8,128)S(1)}, f32[8,512]{1,0:T(8,128)S(1)}, u32[]{:S(2)}, u32[]{:S(2)}) %collective-permute-start.3) | collective-permute-done | bytes 16416 | tf_op jit(solution)/shard_map/ppermute | solution.py:393
  118.6 1.1 shard_map.106
  (21 shorter events, 0.1 us)
Async XLA Ops:
  0.0 3.3 %copy-start.11 = (f32[512]{0:T(512)S(1)}, f32[512]{0:T(512)}, u32[]{:S(2)}) copy-start(f32[512]{0:T(512)} %param.15) | copy-start | bytes 6148
  0.0 3.3 %copy-start.10 = (f32[3,3,512]{2,1,0:T(4,128)S(1)}, f32[3,3,512]{2,1,0:T(4,128)}, u32[]{:S(2)}) copy-start(f32[3,3,512]{2,1,0:T(4,128)} %param.14) | copy-start | bytes 55300
  0.7 1.2 %copy-start = (f32[512,512]{1,0:T(8,128)S(1)}, f32[512,512]{1,0:T(8,128)}, u32[]{:S(2)}) copy-start(f32[512,512]{1,0:T(8,128)} %key_ref.5) | copy-start | bytes 3145732
  2.0 1.2 %copy-start.2 = (f32[512,512]{1,0:T(8,128)S(1)}, f32[512,512]{1,0:T(8,128)}, u32[]{:S(2)}) copy-start(f32[512,512]{1,0:T(8,128)} %value_ref.5) | copy-start | bytes 3145732
  3.2 1.2 %copy-start.1 = (f32[512,512]{1,0:T(8,128)S(1)}, f32[512,512]{1,0:T(8,128)}, u32[]{:S(2)}) copy-start(f32[512,512]{1,0:T(8,128)} %key_ref.5) | copy-start | bytes 3145732
  3.2 1.5 %copy-start.3 = (f32[512,512]{1,0:T(8,128)S(1)}, f32[512,512]{1,0:T(8,128)}, u32[]{:S(2)}) copy-start(f32[512,512]{1,0:T(8,128)} %value_ref.5) | copy-start | bytes 3145732
  3.2 8.9 %collective-permute-start = (f32[3,2,512]{2,1,0:T(2,128)S(1)}, f32[3,2,512]{2,1,0:T(2,128)S(1)}, u32[]{:S(2)}, u32[]{:S(2)}) collective-permute-start(f32[3,2,512]{2,1,0:T(2,128)S(1)} %shard_map.100), channel_id=1, source_target_pairs={{0,4},{4,8},{8,12},{12,16},{16,20},{20,24},{24,28},{28,32},{32,36}... | collective-permute-start | bytes 36872 | tf_op jit(solution)/shard_map/ppermute | solution.py:393
  4.7 1.2 %copy-start.5 = (f32[512,512]{1,0:T(8,128)S(1)}, f32[512,512]{1,0:T(8,128)}, u32[]{:S(2)}) copy-start(f32[512,512]{1,0:T(8,128)} %filter_ref.1) | copy-start | bytes 3145732
  12.4 58.4 %copy-start.6 = (bf16[768,256]{1,0:T(8,128)(2,1)S(1)}, bf16[768,256]{1,0:T(8,128)(2,1)}, u32[]{:S(2)}) copy-start(bf16[768,256]{1,0:T(8,128)(2,1)} %constant.10.clone.fwd) | copy-start | bytes 1179652
  12.4 58.4 %copy-start.7 = (bf16[768,256]{1,0:T(8,128)(2,1)S(1)}, bf16[768,256]{1,0:T(8,128)(2,1)}, u32[]{:S(2)}) copy-start(bf16[768,256]{1,0:T(8,128)(2,1)} %constant.11.clone.bwd) | copy-start | bytes 1179652
  12.4 58.4 %copy-start.8 = (f32[2,33,1,512]{3,2,1,0:T(1,128)S(1)}, f32[2,33,1,512]{3,2,1,0:T(1,128)}, u32[]{:S(2)}) copy-start(f32[2,33,1,512]{3,2,1,0:T(1,128)} %constant.8.clone.twist) | copy-start | bytes 405508
  12.4 58.4 %copy-start.9 = (f32[2,4,1,128]{3,2,1,0:T(1,128)S(1)}, f32[2,4,1,128]{3,2,1,0:T(1,128)}, u32[]{:S(2)}) copy-start(f32[2,4,1,128]{3,2,1,0:T(1,128)} %constant.9.clone.post) | copy-start | bytes 12292
  75.6 5.5 %copy-start.4 = (f32[512,512]{1,0:T(8,128)S(1)}, f32[512,512]{1,0:T(8,128)}, u32[]{:S(2)}) copy-start(f32[512,512]{1,0:T(8,128)} %query_ref.1) | copy-start | bytes 3145732
  75.6 34.4 %all-to-all-start.1 = ((f32[64,8,512]{2,1,0:T(8,128)}), f32[64,8,512]{2,1,0:T(8,128)S(1)}, u32[]{:S(2)}, u32[]{:S(2)}) async-start(f32[64,8,512]{2,1,0:T(8,128)} %shard_map.104), calls=%async_computation.1 | async-start | bytes 2097152 | tf_op jit(solution)/shard_map/all_to_all | solution.py:388
  110.1 5.3 %collective-permute-start.1 = (f32[8,512]{1,0:T(8,128)S(1)}, f32[8,512]{1,0:T(8,128)S(1)}, u32[]{:S(2)}, u32[]{:S(2)}) collective-permute-start(f32[8,512]{1,0:T(8,128)S(1)} %get-tuple-element.8.energy_ref), channel_id=1, source_target_pairs={{0,2},{1,3},{2,0},{3,1},{4,6},{5,7},{6,4},{7,5},{8,10},{9,11},{10,... | collective-permute-start | bytes 49160 | tf_op jit(solution)/shard_map/ppermute | solution.py:393
  111.4 4.0 %collective-permute-start.2 = (f32[8,512]{1,0:T(8,128)S(1)}, f32[8,512]{1,0:T(8,128)S(1)}, u32[]{:S(2)}, u32[]{:S(2)}) collective-permute-start(f32[8,512]{1,0:T(8,128)S(1)} %get-tuple-element.8.energy_ref), channel_id=1, source_target_pairs={{0,1},{1,2},{2,3},{3,0},{4,5},{5,6},{6,7},{7,4},{8,9},{9,10},{10,1... | collective-permute-start | bytes 49160 | tf_op jit(solution)/shard_map/ppermute | solution.py:393
  113.6 4.9 %collective-permute-start.3 = (f32[8,512]{1,0:T(8,128)S(1)}, f32[8,512]{1,0:T(8,128)S(1)}, u32[]{:S(2)}, u32[]{:S(2)}) collective-permute-start(f32[8,512]{1,0:T(8,128)S(1)} %get-tuple-element.8.energy_ref), channel_id=1, source_target_pairs={{0,3},{1,0},{2,1},{3,2},{4,7},{5,4},{6,5},{7,6},{8,11},{9,8},{10,9... | collective-permute-start | bytes 49160 | tf_op jit(solution)/shard_map/ppermute | solution.py:393

commit v4 on v3

--- a/solution.py
+++ b/solution.py
@@ -299,15 +299,32 @@
     else:
         before = x_ref[p - 2 : p + LANE - 2, c : c + LANE]
         one = x_ref[p - 1 : p + LANE - 1, c : c + LANE]
-    return taps[0:1] * tile + taps[1:2] * one + taps[2:3] * before
-
-
-def tail_kernel(query_ref, key_ref, value_ref, out_ref):
-    for g, ref in enumerate((query_ref, key_ref, value_ref)):
-        out_ref[g] = ref[ROWS - 2 :, :]
-
-
-def columns_kernel(filter_ref, key_ref, value_ref, taps_ref, out_ref):
+    return taps[0] * tile + taps[1] * one + taps[2] * before
+
+
+def small_kernel(query_ref, key_ref, value_ref, taps_ref, skip_ref, out_ref, box, taps, skip, sems):
+    height = query_ref.shape[0]
+    copies = [
+        pltpu.make_async_copy(ref.at[pl.ds(height - ROWS, ROWS)], box.at[g], sems.at[g])
+        for g, ref in enumerate((query_ref, key_ref, value_ref))
+    ]
+    copies.append(pltpu.make_async_copy(taps_ref, taps, sems.at[3]))
+    copies.append(pltpu.make_async_copy(skip_ref, skip, sems.at[4]))
+    for copy in copies:
+        copy.start()
+    for copy in copies:
+        copy.wait()
+    for g in range(3):
+        out_ref[2 * g : 2 * g + 2, :] = box[g, ROWS - 2 :, :]
+        out_ref[6 + 3 * g : 9 + 3 * g, :] = taps[g]
+    out_ref[15:16, :] = skip[...]
+
+
+def taps_of(small_ref, g, sl):
+    return [small_ref[6 + 3 * i + g : 7 + 3 * i + g, sl] for i in range(3)]
+
+
+def columns_kernel(filter_ref, key_ref, value_ref, small_ref, out_ref):
     height, width = key_ref.shape
     first = jnp.where(lax.axis_index("seq") == 0, 1.0, 0.0)
     for c in range(0, width, LANE):
@@ -316,30 +333,30 @@
             tile = filter_ref[p : p + LANE, sl]
             if p == 0:
                 row = lax.broadcasted_iota(jnp.int32, tile.shape, 0)
-                tile = tile + jnp.where(row == 0, taps_ref[3, 0:1, sl] * first, 0.0)
+                tile = tile + jnp.where(row == 0, small_ref[15:16, sl] * first, 0.0)
             store_columns(out_ref, c, p, 0, tile)
             if p:
-                k = short_filter(key_ref, None, taps_ref[:, 1, sl], p, c)
-                v = short_filter(value_ref, None, taps_ref[:, 2, sl], p, c)
+                k = short_filter(key_ref, None, taps_of(small_ref, 1, sl), p, c)
+                v = short_filter(value_ref, None, taps_of(small_ref, 2, sl), p, c)
                 store_columns(out_ref, c, p, ROWS, k * v)
 
 
-def edge_kernel(key_ref, value_ref, halo_ref, taps_ref, cols_ref, out_ref):
+def edge_kernel(key_ref, value_ref, halo_ref, small_ref, cols_ref, out_ref):
     del cols_ref
     width = key_ref.shape[1]
     for c in range(0, width, LANE):
         sl = slice(c, c + LANE)
-        k = short_filter(key_ref, halo_ref[1, :, sl], taps_ref[:, 1, sl], 0, c)
-        v = short_filter(value_ref, halo_ref[2, :, sl], taps_ref[:, 2, sl], 0, c)
+        k = short_filter(key_ref, halo_ref[2 : 4, sl], taps_of(small_ref, 1, sl), 0, c)
+        v = short_filter(value_ref, halo_ref[4 : 6, sl], taps_of(small_ref, 2, sl), 0, c)
         store_columns(out_ref, c, 0, ROWS, k * v)
 
 
-def query_kernel(query_ref, halo_ref, taps_ref, out_ref):
+def query_kernel(query_ref, halo_ref, small_ref, out_ref):
     height, width = query_ref.shape
     for c in range(0, width, LANE):
         sl = slice(c, c + LANE)
         for p in range(0, height, LANE):
-            q = short_filter(query_ref, halo_ref[0, :, sl], taps_ref[:, 0, sl], p, c)
+            q = short_filter(query_ref, halo_ref[0 : 2, sl], taps_of(small_ref, 0, sl), p, c)
             out_ref[sl, p : p + LANE] = q.T
 
 
@@ -401,29 +418,31 @@
     pair = jax.ShapeDtypeStruct((shards, 2 * ROWS, height), jnp.float32)
     cube = jax.ShapeDtypeStruct((shards, ROWS, height), jnp.float32)
 
-    direct = jnp.broadcast_to(skip_gain, (1, 3, width))
-    taps = jnp.concatenate([short_weight, direct])
-    last = pl.BlockSpec((ROWS, width), lambda i: (height // ROWS - 1, 0))
-    tail = call(
-        tail_kernel,
-        jax.ShapeDtypeStruct((3, 2, width), jnp.float32),
-        proj_query[height - ROWS :, :], proj_key, proj_value,
-        grid=(1,),
-        ins=[pl.BlockSpec((ROWS, width), lambda i: (0, 0)), last, last],
-        out_specs=pl.BlockSpec((3, 2, width), lambda i: (0, 0, 0)),
+    small = call(
+        small_kernel,
+        jax.ShapeDtypeStruct((2 * ROWS, width), jnp.float32),
+        proj_query, proj_key, proj_value, short_weight, skip_gain[None, :],
+        ins=[HB] * 5,
+        scratch=[
+            pltpu.VMEM((3, ROWS, width), jnp.float32),
+            pltpu.VMEM((3, 3, width), jnp.float32),
+            pltpu.VMEM((1, width), jnp.float32),
+            pltpu.SemaphoreType.DMA((5,)),
+        ],
         moved=100_000,
-    )
-    halo = shifted(tail, "seq", 1)
+        vmem=60,
+    )
+    halo = shifted(small, "seq", 1)
     cols = call(
-        columns_kernel, pair, long_filter, proj_key, proj_value, taps
+        columns_kernel, pair, long_filter, proj_key, proj_value, small
     )
     cols = call(
-        edge_kernel, pair, proj_key, proj_value, halo, taps, cols,
+        edge_kernel, pair, proj_key, proj_value, halo, small, cols,
         aliases={4: 0},
         moved=1_000_000,
     )
     cols = exchange(cols)
-    query_t = call(query_kernel, block, proj_query, halo, taps)
+    query_t = call(query_kernel, block, proj_query, halo, small)
 
     conv_cols = call(
         functools.partial(convolve_kernel, 1.0 / (shards * height)),

time: 120 us -> 119 us (level)
  local copies, waits for them, and re-layouts: 5.84 us -> 1.01 us
  waiting for transfers between devices: 39.1 us -> 41.2 us
  Pallas kernels: 7.3 us -> 8.87 us
    unnamed x24 -> x20, local copies, waits for them, and re-layouts: 5.1 us -> 1.01 us
    ppermute x4, waiting for transfers between devices: 10.6 us -> 12.7 us  [shifted(): lax.ppermute(value, axis, [(i, (i + steps) % count) for i in range(count)])]
    pallas_call x7, Pallas kernels: 7.3 us -> 8.87 us  [call(): pl.pallas_call(kernel, out_shape=outs, grid=grid, in_specs=ins or [VM] *...]
where the time goes in v4:
time: 119 us
  blocking collectives  58.3 us (49%)
  waiting for transfers between devices  41.2 us (35%)
  starting transfers between devices  9.05 us (8%)
  Pallas kernels  8.87 us (7%)
    all_to_all x1, blocking collectives, exchange(): lax.all_to_all(values, 'seq', split_axis=0, concat_axis=0, tiled=True)  58.3 us
    all_to_all x1, waiting for transfers between devices, exchange(): lax.all_to_all(values, 'seq', split_axis=0, concat_axis=0, tiled=True)  28.5 us
    ppermute x4, waiting for transfers between devices, shifted(): lax.ppermute(value, axis, [(i, (i + steps) % count) for i in range(count)])  12.7 us
    pallas_call x7, Pallas kernels, call(): pl.pallas_call(kernel, out_shape=outs, grid=grid, in_specs=ins or [VM] *...  8.87 us
    all_to_all x1, starting transfers between devices, exchange(): lax.all_to_all(values, 'seq', split_axis=0, concat_axis=0, tiled=True)  5.47 us
    ppermute x4, starting transfers between devices, shifted(): lax.ppermute(value, axis, [(i, (i + steps) % count) for i in range(count)])  3.59 us
  transfers between devices with their start and end apart: 5, of which 4 were waited for; matrix products, arithmetic and copies ran while one was open for 0% of the time, Pallas kernels for 1%

profile of v4, /device:TPU:24, one launch (start us, length us, event | category | flops | bytes accessed | tf_op | source)
XLA Modules:
  0.0 118.5 jit_solution(17741272928941670656)
XLA Ops:
  0.0 1.6 %shard_map.100.small_ref = f32[16,512]{1,0:T(8,128)} custom-call(f32[512,512]{1,0:T(8,128)} %query_ref.3, f32[512,512]{1,0:T(8,128)} %key_ref.5, f32[512,512]{1,0:T(8,128)} %value_ref.5, f32[3,3,512]{2,1,0:T(4,128)} %taps_ref.1, f32[1,512]{1,0:T(1,128)} %bitcast.3), custom_call_target="tpu_custom_call" | custom-call | flops 10000000 | bytes 100000 | tf_op jit(solution)/shard_map/pallas_call | solution.py:391
  1.6 0.1 collective-permute-start
  1.7 0.2 copy-done.3
  2.0 0.8 copy-done.4
  2.7 0.6 shard_map.102.cols_ref
  3.3 7.7 %collective-permute-done.halo_ref = f32[16,512]{1,0:T(8,128)S(1)} collective-permute-done((f32[16,512]{1,0:T(8,128)}, f32[16,512]{1,0:T(8,128)S(1)}, u32[]{:S(2)}, u32[]{:S(2)}) %collective-permute-start) | collective-permute-done | bytes 32800 | tf_op jit(solution)/shard_map/ppermute | solution.py:410
  11.0 0.2 shard_map.103
  11.2 0.0 copy-start.6
  11.3 0.0 copy-start.7
  11.3 0.0 copy-start.8
  11.3 0.0 copy-start.9
  11.3 58.3 %all_to_all.10.cols = f32[64,16,512]{2,1,0:T(8,128)S(1)} all-to-all(f32[64,16,512]{2,1,0:T(8,128)S(1)} %shard_map.103), channel_id=1, replica_groups=mesh['seq'=64,'chan'=4] {'seq'}, dimensions={0} | all-to-all | bytes 4194304 | tf_op jit(solution)/shard_map/all_to_all | solution.py:405
  69.7 4.8 %shard_map.104 = f32[64,8,512]{2,1,0:T(8,128)} custom-call(f32[64,16,512]{2,1,0:T(8,128)S(1)} %all_to_all.10.cols, f32[2,33,1,512]{3,2,1,0:T(1,128)S(1)} %copy-done.8, f32[2,4,1,128]{3,2,1,0:T(1,128)S(1)} %copy-done.9, bf16[768,256]{1,0:T(8,128)(2,1)S(1)} %copy-done.6, bf16[768,256]{1,0:T(8,128)(2,1)S(1)} %copy-done.7), custom_call_target="tpu_custom_call" | custom-call | flops 3000000000 | bytes 4000000 | tf_op jit(solution)/shard_map/pallas_call | solution.py:391
  74.4 5.5 %all-to-all-start.1 = ((f32[64,8,512]{2,1,0:T(8,128)}), f32[64,8,512]{2,1,0:T(8,128)S(1)}, u32[]{:S(2)}, u32[]{:S(2)}) async-start(f32[64,8,512]{2,1,0:T(8,128)} %shard_map.104), calls=%async_computation.1 | async-start | bytes 2097152 | tf_op jit(solution)/shard_map/all_to_all | solution.py:405
  79.9 0.4 shard_map.101.query_ref
  80.3 28.5 %all-to-all-done.1 = f32[64,8,512]{2,1,0:T(8,128)S(1)} async-done(((f32[64,8,512]{2,1,0:T(8,128)}), f32[64,8,512]{2,1,0:T(8,128)S(1)}, u32[]{:S(2)}, u32[]{:S(2)}) %all-to-all-start.1) | async-done | bytes 1048608 | tf_op jit(solution)/shard_map/all_to_all | solution.py:405
  108.8 0.1 shard_map.105
  108.9 1.3 %collective-permute-start.1 = (f32[8,512]{1,0:T(8,128)S(1)}, f32[8,512]{1,0:T(8,128)S(1)}, u32[]{:S(2)}, u32[]{:S(2)}) collective-permute-start(f32[8,512]{1,0:T(8,128)S(1)} %get-tuple-element.8.energy_ref), channel_id=1, source_target_pairs={{0,2},{1,3},{2,0},{3,1},{4,6},{5,7},{6,4},{7,5},{8,10},{9,11},{10,... | collective-permute-start | bytes 49160 | tf_op jit(solution)/shard_map/ppermute | solution.py:410
  110.3 2.2 %collective-permute-start.2 = (f32[8,512]{1,0:T(8,128)S(1)}, f32[8,512]{1,0:T(8,128)S(1)}, u32[]{:S(2)}, u32[]{:S(2)}) collective-permute-start(f32[8,512]{1,0:T(8,128)S(1)} %get-tuple-element.8.energy_ref), channel_id=1, source_target_pairs={{0,1},{1,2},{2,3},{3,0},{4,5},{5,6},{6,7},{7,4},{8,9},{9,10},{10,1... | collective-permute-start | bytes 49160 | tf_op jit(solution)/shard_map/ppermute | solution.py:410
  112.4 0.0 collective-permute-start.3
  112.4 1.8 %collective-permute-done.1.e1 = f32[8,512]{1,0:T(8,128)S(1)} collective-permute-done((f32[8,512]{1,0:T(8,128)S(1)}, f32[8,512]{1,0:T(8,128)S(1)}, u32[]{:S(2)}, u32[]{:S(2)}) %collective-permute-start.1) | collective-permute-done | bytes 16416 | tf_op jit(solution)/shard_map/ppermute | solution.py:410
  114.3 0.0 collective-permute-done.2.e2
  114.3 3.1 %collective-permute-done.3.e3 = f32[8,512]{1,0:T(8,128)S(1)} collective-permute-done((f32[8,512]{1,0:T(8,128)S(1)}, f32[8,512]{1,0:T(8,128)S(1)}, u32[]{:S(2)}, u32[]{:S(2)}) %collective-permute-start.3) | collective-permute-done | bytes 16416 | tf_op jit(solution)/shard_map/ppermute | solution.py:410
  117.4 1.1 shard_map.106
  (14 shorter events, 0.0 us)
Async XLA Ops:
  0.0 1.7 %copy-start = (f32[512,512]{1,0:T(8,128)S(1)}, f32[512,512]{1,0:T(8,128)}, u32[]{:S(2)}) copy-start(f32[512,512]{1,0:T(8,128)} %key_ref.5) | copy-start | bytes 3145732
  0.0 1.7 %copy-start.1 = (f32[512,512]{1,0:T(8,128)S(1)}, f32[512,512]{1,0:T(8,128)}, u32[]{:S(2)}) copy-start(f32[512,512]{1,0:T(8,128)} %value_ref.5) | copy-start | bytes 3145732
  0.0 1.9 %copy-start.3 = (f32[512,512]{1,0:T(8,128)S(1)}, f32[512,512]{1,0:T(8,128)}, u32[]{:S(2)}) copy-start(f32[512,512]{1,0:T(8,128)} %filter_ref.1) | copy-start | bytes 3145732
  1.6 9.4 %collective-permute-start = (f32[16,512]{1,0:T(8,128)}, f32[16,512]{1,0:T(8,128)S(1)}, u32[]{:S(2)}, u32[]{:S(2)}) collective-permute-start(f32[16,512]{1,0:T(8,128)} %shard_map.100.small_ref), channel_id=1, source_target_pairs={{0,4},{4,8},{8,12},{12,16},{16,20},{20,24},{24,28},{28,32},{32,36}... | collective-permute-start | bytes 98312 | tf_op jit(solution)/shard_map/ppermute | solution.py:410
  1.9 0.8 copy-start.4
  2.7 8.3 %copy-start.5 = (f32[16,512]{1,0:T(8,128)S(1)}, f32[16,512]{1,0:T(8,128)}, u32[]{:S(2)}) copy-start(f32[16,512]{1,0:T(8,128)} %shard_map.100.small_ref) | copy-start | bytes 98308
  11.2 58.4 %copy-start.6 = (bf16[768,256]{1,0:T(8,128)(2,1)S(1)}, bf16[768,256]{1,0:T(8,128)(2,1)}, u32[]{:S(2)}) copy-start(bf16[768,256]{1,0:T(8,128)(2,1)} %constant.10.clone.fwd) | copy-start | bytes 1179652
  11.3 58.4 %copy-start.7 = (bf16[768,256]{1,0:T(8,128)(2,1)S(1)}, bf16[768,256]{1,0:T(8,128)(2,1)}, u32[]{:S(2)}) copy-start(bf16[768,256]{1,0:T(8,128)(2,1)} %constant.11.clone.bwd) | copy-start | bytes 1179652
  11.3 58.4 %copy-start.8 = (f32[2,33,1,512]{3,2,1,0:T(1,128)S(1)}, f32[2,33,1,512]{3,2,1,0:T(1,128)}, u32[]{:S(2)}) copy-start(f32[2,33,1,512]{3,2,1,0:T(1,128)} %constant.8.clone.twist) | copy-start | bytes 405508
  11.3 58.4 %copy-start.9 = (f32[2,4,1,128]{3,2,1,0:T(1,128)S(1)}, f32[2,4,1,128]{3,2,1,0:T(1,128)}, u32[]{:S(2)}) copy-start(f32[2,4,1,128]{3,2,1,0:T(1,128)} %constant.9.clone.post) | copy-start | bytes 12292
  74.4 5.5 %copy-start.2 = (f32[512,512]{1,0:T(8,128)S(1)}, f32[512,512]{1,0:T(8,128)}, u32[]{:S(2)}) copy-start(f32[512,512]{1,0:T(8,128)} %query_ref.3) | copy-start | bytes 3145732
  74.4 34.4 %all-to-all-start.1 = ((f32[64,8,512]{2,1,0:T(8,128)}), f32[64,8,512]{2,1,0:T(8,128)S(1)}, u32[]{:S(2)}, u32[]{:S(2)}) async-start(f32[64,8,512]{2,1,0:T(8,128)} %shard_map.104), calls=%async_computation.1 | async-start | bytes 2097152 | tf_op jit(solution)/shard_map/all_to_all | solution.py:405
  108.9 5.3 %collective-permute-start.1 = (f32[8,512]{1,0:T(8,128)S(1)}, f32[8,512]{1,0:T(8,128)S(1)}, u32[]{:S(2)}, u32[]{:S(2)}) collective-permute-start(f32[8,512]{1,0:T(8,128)S(1)} %get-tuple-element.8.energy_ref), channel_id=1, source_target_pairs={{0,2},{1,3},{2,0},{3,1},{4,6},{5,7},{6,4},{7,5},{8,10},{9,11},{10,... | collective-permute-start | bytes 49160 | tf_op jit(solution)/shard_map/ppermute | solution.py:410
  110.3 4.0 %collective-permute-start.2 = (f32[8,512]{1,0:T(8,128)S(1)}, f32[8,512]{1,0:T(8,128)S(1)}, u32[]{:S(2)}, u32[]{:S(2)}) collective-permute-start(f32[8,512]{1,0:T(8,128)S(1)} %get-tuple-element.8.energy_ref), channel_id=1, source_target_pairs={{0,1},{1,2},{2,3},{3,0},{4,5},{5,6},{6,7},{7,4},{8,9},{9,10},{10,1... | collective-permute-start | bytes 49160 | tf_op jit(solution)/shard_map/ppermute | solution.py:410
  112.4 4.9 %collective-permute-start.3 = (f32[8,512]{1,0:T(8,128)S(1)}, f32[8,512]{1,0:T(8,128)S(1)}, u32[]{:S(2)}, u32[]{:S(2)}) collective-permute-start(f32[8,512]{1,0:T(8,128)S(1)} %get-tuple-element.8.energy_ref), channel_id=1, source_target_pairs={{0,3},{1,0},{2,1},{3,2},{4,7},{5,4},{6,5},{7,6},{8,11},{9,8},{10,9... | collective-permute-start | bytes 49160 | tf_op jit(solution)/shard_map/ppermute | solution.py:410

commit v5 on v4

--- a/solution.py
+++ b/solution.py
@@ -302,7 +302,7 @@
     return taps[0] * tile + taps[1] * one + taps[2] * before
 
 
-def small_kernel(query_ref, key_ref, value_ref, taps_ref, skip_ref, out_ref, box, taps, skip, sems):
+def small_kernel(query_ref, key_ref, value_ref, taps_ref, skip_ref, ends_ref, out_ref, box, taps, skip, sems):
     height = query_ref.shape[0]
     copies = [
         pltpu.make_async_copy(ref.at[pl.ds(height - ROWS, ROWS)], box.at[g], sems.at[g])
@@ -315,13 +315,13 @@
     for copy in copies:
         copy.wait()
     for g in range(3):
-        out_ref[2 * g : 2 * g + 2, :] = box[g, ROWS - 2 :, :]
-        out_ref[6 + 3 * g : 9 + 3 * g, :] = taps[g]
-    out_ref[15:16, :] = skip[...]
+        ends_ref[2 * g : 2 * g + 2, :] = box[g, ROWS - 2 :, :]
+        out_ref[3 * g : 3 * g + 3, :] = taps[g]
+    out_ref[9:10, :] = skip[...]
 
 
 def taps_of(small_ref, g, sl):
-    return [small_ref[6 + 3 * i + g : 7 + 3 * i + g, sl] for i in range(3)]
+    return [small_ref[3 * i + g : 3 * i + g + 1, sl] for i in range(3)]
 
 
 def columns_kernel(filter_ref, key_ref, value_ref, small_ref, out_ref):
@@ -333,7 +333,7 @@
             tile = filter_ref[p : p + LANE, sl]
             if p == 0:
                 row = lax.broadcasted_iota(jnp.int32, tile.shape, 0)
-                tile = tile + jnp.where(row == 0, small_ref[15:16, sl] * first, 0.0)
+                tile = tile + jnp.where(row == 0, small_ref[9:10, sl] * first, 0.0)
             store_columns(out_ref, c, p, 0, tile)
             if p:
                 k = short_filter(key_ref, None, taps_of(small_ref, 1, sl), p, c)
@@ -367,13 +367,13 @@
         value = query_ref[r : r + ROWS, :] * conv_ref[r : r + ROWS, :]
         response_ref[r : r + ROWS, :] = value
         total = total + value * value
-    energy_ref[...] = jnp.broadcast_to(jnp.sum(total, axis=0, keepdims=True), energy_ref.shape)
+    energy_ref[...] = jnp.sum(total, axis=0, keepdims=True)
 
 
 def norm_kernel(channels, response_ref, energy_ref, e1, e2, e3, out_ref, box, sems):
     height, width = response_ref.shape
     mean = (energy_ref[...] + e1[...] + e2[...] + e3[...]) / channels
-    gain = 1.0 / jnp.sqrt(mean[0:1] + 1e-06)
+    gain = 1.0 / jnp.sqrt(mean + 1e-06)
     copies = []
     for i, p in enumerate(range(0, width, LANE)):
         for c in range(0, height, LANE):
@@ -418,9 +418,12 @@
     pair = jax.ShapeDtypeStruct((shards, 2 * ROWS, height), jnp.float32)
     cube = jax.ShapeDtypeStruct((shards, ROWS, height), jnp.float32)
 
-    small = call(
+    ends, small = call(
         small_kernel,
-        jax.ShapeDtypeStruct((2 * ROWS, width), jnp.float32),
+        (
+            jax.ShapeDtypeStruct((6, width), jnp.float32),
+            jax.ShapeDtypeStruct((10, width), jnp.float32),
+        ),
         proj_query, proj_key, proj_value, short_weight, skip_gain[None, :],
         ins=[HB] * 5,
         scratch=[
@@ -432,7 +435,7 @@
         moved=100_000,
         vmem=60,
     )
-    halo = shifted(small, "seq", 1)
+    halo = shifted(ends, "seq", 1)
     cols = call(
         columns_kernel, pair, long_filter, proj_key, proj_value, small
     )
@@ -461,7 +464,7 @@
     conv = exchange(conv_cols).reshape(width, height)
     response, energy = call(
         response_kernel,
-        (block, jax.ShapeDtypeStruct((ROWS, height), jnp.float32)),
+        (block, jax.ShapeDtypeStruct((1, height), jnp.float32)),
         query_t, conv,
     )
     others = [shifted(energy, "chan", k) for k in (2, 1, 3)]

time: 119 us -> 119 us (level)
  no operation moved by 1% of the time
where the time goes in v5:
time: 119 us; the launch traced here: 118 us
  blocking collectives  58.3 us (49%)
  waiting for transfers between devices  40.8 us (34%)
  starting transfers between devices  9.05 us (8%)
  Pallas kernels  8.9 us (7%)
    all_to_all x1, blocking collectives, exchange(): lax.all_to_all(values, 'seq', split_axis=0, concat_axis=0, tiled=True)  58.3 us
    all_to_all x1, waiting for transfers between devices, exchange(): lax.all_to_all(values, 'seq', split_axis=0, concat_axis=0, tiled=True)  28.5 us
    ppermute x4, waiting for transfers between devices, shifted(): lax.ppermute(value, axis, [(i, (i + steps) % count) for i in range(count)])  12.3 us
    pallas_call x7, Pallas kernels, call(): pl.pallas_call(kernel, out_shape=outs, grid=grid, in_specs=ins or [VM] *...  8.9 us
    all_to_all x1, starting transfers between devices, exchange(): lax.all_to_all(values, 'seq', split_axis=0, concat_axis=0, tiled=True)  5.47 us
    ppermute x4, starting transfers between devices, shifted(): lax.ppermute(value, axis, [(i, (i + steps) % count) for i in range(count)])  3.59 us
  transfers between devices with their start and end apart: 5, of which 4 were waited for; matrix products, arithmetic and copies ran while one was open for 0% of the time, Pallas kernels for 1%

profile of v5, /device:TPU:24, one launch (start us, length us, event | category | flops | bytes accessed | tf_op | source)
XLA Modules:
  0.0 118.2 jit_solution(2161461744018037691)
XLA Ops:
  0.0 1.6 %shard_map.100 = (f32[6,512]{1,0:T(8,128)}, f32[10,512]{1,0:T(8,128)}) custom-call(f32[512,512]{1,0:T(8,128)} %query_ref.3, f32[512,512]{1,0:T(8,128)} %key_ref.5, f32[512,512]{1,0:T(8,128)} %value_ref.5, f32[3,3,512]{2,1,0:T(4,128)} %taps_ref.1, f32[1,512]{1,0:T(1,128)} %bitcast.3), custom_call_target="tpu_custom_call" | custom-call | flops 10000000 | bytes 100000 | tf_op jit(solution)/shard_map/pallas_call | solution.py:391
  1.6 0.1 collective-permute-start
  1.7 0.2 copy-done.3
  2.0 0.8 copy-done.4
  2.7 0.6 shard_map.102.cols_ref
  3.3 7.5 %collective-permute-done.halo_ref = f32[6,512]{1,0:T(8,128)S(1)} collective-permute-done((f32[6,512]{1,0:T(8,128)}, f32[6,512]{1,0:T(8,128)S(1)}, u32[]{:S(2)}, u32[]{:S(2)}) %collective-permute-start) | collective-permute-done | bytes 12320 | tf_op jit(solution)/shard_map/ppermute | solution.py:410
  10.8 0.2 shard_map.103
  11.1 0.0 copy-start.6
  11.1 0.0 copy-start.7
  11.1 0.0 copy-start.8
  11.1 0.0 copy-start.9
  11.1 58.3 %all_to_all.10.cols = f32[64,16,512]{2,1,0:T(8,128)S(1)} all-to-all(f32[64,16,512]{2,1,0:T(8,128)S(1)} %shard_map.103), channel_id=1, replica_groups=mesh['seq'=64,'chan'=4] {'seq'}, dimensions={0} | all-to-all | bytes 4194304 | tf_op jit(solution)/shard_map/all_to_all | solution.py:405
  69.5 4.8 %shard_map.104 = f32[64,8,512]{2,1,0:T(8,128)} custom-call(f32[64,16,512]{2,1,0:T(8,128)S(1)} %all_to_all.10.cols, f32[2,33,1,512]{3,2,1,0:T(1,128)S(1)} %copy-done.8, f32[2,4,1,128]{3,2,1,0:T(1,128)S(1)} %copy-done.9, bf16[768,256]{1,0:T(8,128)(2,1)S(1)} %copy-done.6, bf16[768,256]{1,0:T(8,128)(2,1)S(1)} %copy-done.7), custom_call_target="tpu_custom_call" | custom-call | flops 3000000000 | bytes 4000000 | tf_op jit(solution)/shard_map/pallas_call | solution.py:391
  74.3 5.5 %all-to-all-start.1 = ((f32[64,8,512]{2,1,0:T(8,128)}), f32[64,8,512]{2,1,0:T(8,128)S(1)}, u32[]{:S(2)}, u32[]{:S(2)}) async-start(f32[64,8,512]{2,1,0:T(8,128)} %shard_map.104), calls=%async_computation.1 | async-start | bytes 2097152 | tf_op jit(solution)/shard_map/all_to_all | solution.py:405
  79.8 0.4 shard_map.101.query_ref
  80.2 28.5 %all-to-all-done.1 = f32[64,8,512]{2,1,0:T(8,128)S(1)} async-done(((f32[64,8,512]{2,1,0:T(8,128)}), f32[64,8,512]{2,1,0:T(8,128)S(1)}, u32[]{:S(2)}, u32[]{:S(2)}) %all-to-all-start.1) | async-done | bytes 1048608 | tf_op jit(solution)/shard_map/all_to_all | solution.py:405
  108.7 0.1 shard_map.105
  108.8 1.3 %collective-permute-start.1 = (f32[1,512]{1,0:T(1,128)S(1)}, f32[1,512]{1,0:T(1,128)S(1)}, u32[]{:S(2)}, u32[]{:S(2)}) collective-permute-start(f32[1,512]{1,0:T(1,128)S(1)} %get-tuple-element.12.energy_ref), channel_id=1, source_target_pairs={{0,2},{1,3},{2,0},{3,1},{4,6},{5,7},{6,4},{7,5},{8,10},{9,11},{10,... | collective-permute-start | bytes 6152 | tf_op jit(solution)/shard_map/ppermute | solution.py:410
  110.1 2.2 %collective-permute-start.2 = (f32[1,512]{1,0:T(1,128)S(1)}, f32[1,512]{1,0:T(1,128)S(1)}, u32[]{:S(2)}, u32[]{:S(2)}) collective-permute-start(f32[1,512]{1,0:T(1,128)S(1)} %get-tuple-element.12.energy_ref), channel_id=1, source_target_pairs={{0,1},{1,2},{2,3},{3,0},{4,5},{5,6},{6,7},{7,4},{8,9},{9,10},{10,1... | collective-permute-start | bytes 6152 | tf_op jit(solution)/shard_map/ppermute | solution.py:410
  112.3 0.0 collective-permute-start.3
  112.3 1.7 %collective-permute-done.1.e1 = f32[1,512]{1,0:T(1,128)S(1)} collective-permute-done((f32[1,512]{1,0:T(1,128)S(1)}, f32[1,512]{1,0:T(1,128)S(1)}, u32[]{:S(2)}, u32[]{:S(2)}) %collective-permute-start.1) | collective-permute-done | bytes 2080 | tf_op jit(solution)/shard_map/ppermute | solution.py:410
  114.0 0.0 collective-permute-done.2.e2
  114.0 3.1 %collective-permute-done.3.e3 = f32[1,512]{1,0:T(1,128)S(1)} collective-permute-done((f32[1,512]{1,0:T(1,128)S(1)}, f32[1,512]{1,0:T(1,128)S(1)}, u32[]{:S(2)}, u32[]{:S(2)}) %collective-permute-start.3) | collective-permute-done | bytes 2080 | tf_op jit(solution)/shard_map/ppermute | solution.py:410
  117.1 1.1 shard_map.106
  (14 shorter events, 0.0 us)
Async XLA Ops:
  0.0 1.7 %copy-start = (f32[512,512]{1,0:T(8,128)S(1)}, f32[512,512]{1,0:T(8,128)}, u32[]{:S(2)}) copy-start(f32[512,512]{1,0:T(8,128)} %key_ref.5) | copy-start | bytes 3145732
  0.0 1.7 %copy-start.1 = (f32[512,512]{1,0:T(8,128)S(1)}, f32[512,512]{1,0:T(8,128)}, u32[]{:S(2)}) copy-start(f32[512,512]{1,0:T(8,128)} %value_ref.5) | copy-start | bytes 3145732
  0.0 1.9 %copy-start.3 = (f32[512,512]{1,0:T(8,128)S(1)}, f32[512,512]{1,0:T(8,128)}, u32[]{:S(2)}) copy-start(f32[512,512]{1,0:T(8,128)} %filter_ref.1) | copy-start | bytes 3145732
  1.6 9.2 %collective-permute-start = (f32[6,512]{1,0:T(8,128)}, f32[6,512]{1,0:T(8,128)S(1)}, u32[]{:S(2)}, u32[]{:S(2)}) collective-permute-start(f32[6,512]{1,0:T(8,128)} %get-tuple-element.9), channel_id=1, source_target_pairs={{0,4},{4,8},{8,12},{12,16},{16,20},{20,24},{24,28},{28,32},{32,36}... | collective-permute-start | bytes 36872 | tf_op jit(solution)/shard_map/ppermute | solution.py:410
  2.0 0.8 copy-start.4
  11.1 58.4 %copy-start.6 = (bf16[768,256]{1,0:T(8,128)(2,1)S(1)}, bf16[768,256]{1,0:T(8,128)(2,1)}, u32[]{:S(2)}) copy-start(bf16[768,256]{1,0:T(8,128)(2,1)} %constant.10.clone.fwd) | copy-start | bytes 1179652
  11.1 58.4 %copy-start.7 = (bf16[768,256]{1,0:T(8,128)(2,1)S(1)}, bf16[768,256]{1,0:T(8,128)(2,1)}, u32[]{:S(2)}) copy-start(bf16[768,256]{1,0:T(8,128)(2,1)} %constant.11.clone.bwd) | copy-start | bytes 1179652
  11.1 58.4 %copy-start.8 = (f32[2,33,1,512]{3,2,1,0:T(1,128)S(1)}, f32[2,33,1,512]{3,2,1,0:T(1,128)}, u32[]{:S(2)}) copy-start(f32[2,33,1,512]{3,2,1,0:T(1,128)} %constant.8.clone.twist) | copy-start | bytes 405508
  11.1 58.4 %copy-start.9 = (f32[2,4,1,128]{3,2,1,0:T(1,128)S(1)}, f32[2,4,1,128]{3,2,1,0:T(1,128)}, u32[]{:S(2)}) copy-start(f32[2,4,1,128]{3,2,1,0:T(1,128)} %constant.9.clone.post) | copy-start | bytes 12292
  74.3 5.5 %copy-start.2 = (f32[512,512]{1,0:T(8,128)S(1)}, f32[512,512]{1,0:T(8,128)}, u32[]{:S(2)}) copy-start(f32[512,512]{1,0:T(8,128)} %query_ref.3) | copy-start | bytes 3145732
  74.3 5.5 %copy-start.5 = (f32[10,512]{1,0:T(8,128)S(1)}, f32[10,512]{1,0:T(8,128)}, u32[]{:S(2)}) copy-start(f32[10,512]{1,0:T(8,128)} %get-tuple-element.10.small_ref) | copy-start | bytes 61444
  74.3 34.4 %all-to-all-start.1 = ((f32[64,8,512]{2,1,0:T(8,128)}), f32[64,8,512]{2,1,0:T(8,128)S(1)}, u32[]{:S(2)}, u32[]{:S(2)}) async-start(f32[64,8,512]{2,1,0:T(8,128)} %shard_map.104), calls=%async_computation.1 | async-start | bytes 2097152 | tf_op jit(solution)/shard_map/all_to_all | solution.py:405
  108.8 5.2 %collective-permute-start.1 = (f32[1,512]{1,0:T(1,128)S(1)}, f32[1,512]{1,0:T(1,128)S(1)}, u32[]{:S(2)}, u32[]{:S(2)}) collective-permute-start(f32[1,512]{1,0:T(1,128)S(1)} %get-tuple-element.12.energy_ref), channel_id=1, source_target_pairs={{0,2},{1,3},{2,0},{3,1},{4,6},{5,7},{6,4},{7,5},{8,10},{9,11},{10,... | collective-permute-start | bytes 6152 | tf_op jit(solution)/shard_map/ppermute | solution.py:410
  110.1 3.9 %collective-permute-start.2 = (f32[1,512]{1,0:T(1,128)S(1)}, f32[1,512]{1,0:T(1,128)S(1)}, u32[]{:S(2)}, u32[]{:S(2)}) collective-permute-start(f32[1,512]{1,0:T(1,128)S(1)} %get-tuple-element.12.energy_ref), channel_id=1, source_target_pairs={{0,1},{1,2},{2,3},{3,0},{4,5},{5,6},{6,7},{7,4},{8,9},{9,10},{10,1... | collective-permute-start | bytes 6152 | tf_op jit(solution)/shard_map/ppermute | solution.py:410
  112.3 4.8 %collective-permute-start.3 = (f32[1,512]{1,0:T(1,128)S(1)}, f32[1,512]{1,0:T(1,128)S(1)}, u32[]{:S(2)}, u32[]{:S(2)}) collective-permute-start(f32[1,512]{1,0:T(1,128)S(1)} %get-tuple-element.12.energy_ref), channel_id=1, source_target_pairs={{0,3},{1,0},{2,1},{3,2},{4,7},{5,4},{6,5},{7,6},{8,11},{9,8},{10,9... | collective-permute-start | bytes 6152 | tf_op jit(solution)/shard_map/ppermute | solution.py:410
